TPU v7x, 32 devices: a whole 2x2x4 slice. The times are simulated.
32 devices in a mesh: grp: 4 (over z), tile: 8 (over y, x, core).
Axes of the slice: x: 2, y: 2, z: 4, core: 2. Of those that a mesh axis runs over, the one named last changes fastest.
Arguments:
- speed: float32 [32, 2, 32, 128], P('tile'), may hold values from 0.15 to 0.4
- density: float32 [32, 2, 32, 128], P('tile'), may hold values from 1 to 3
- fwd_state: bfloat16 [32, 4, 8, 32, 128], P(('grp', 'tile')), may hold values from -6 to 6
- adj_state: bfloat16 [32, 4, 8, 32, 128], P(('grp', 'tile')), may hold values from -6 to 6
- aperture: int32 [32, 4], P(('grp', 'tile')), may hold values from 0 to 31, as said below
- src_pos: int32 [32, 3], P(('grp', 'tile')), may hold values from 0 to 127, as said below
- wavelet: float32 [32, 4], P(('grp', 'tile')), may hold values from -15 to 15
- rec_pos: int32 [32, 8, 2], P(('grp', 'tile')), may hold values from 0 to 127, as said below
- residual: float32 [32, 4, 8], P(('grp', 'tile')), may hold values from -6 to 6
Outputs:
- grad_speed: float32 [32, 2, 32, 128], P('tile')
- grad_density: float32 [32, 2, 32, 128], P('tile')
Inputs may be any that keep to these rules, and one draw needn't show every extreme that they name: `aperture`: row s is (c + j) * 4 + e for j = 0 .. 3, with one c in 0 .. 4 and one e in 0 .. 3 for each shot, so a shot takes exactly one tile from each of 4 owners. `src_pos`: columns are x in 0 .. 7, y in 0 .. 31, z in 0 .. 127. `rec_pos`: columns are y in 0 .. 31 and z in 0 .. 127.
All inputs are finite; a program needn't handle non-finite values.
Results may differ from a plain program's by a relative error of at most 0.0003.
Values sent between devices are 32-bit elements; how exact they have to be, the bound alone decides.
No kernel may reach another device: no remote copies, remote signals or barrier semaphores. Data moves between devices by JAX's collectives and lax.ppermute only.
A program may use at most 64 MiB of HBM per device.

v0:
```python
import functools
import math

import jax
import jax.numpy as jnp
from jax import lax
from jax.experimental import pallas as pl
from jax.experimental.pallas import tpu as pltpu
from jax.sharding import PartitionSpec as P

COEF = (1225.0 / 1024.0, -245.0 / 3072.0, 49.0 / 5120.0, -5.0 / 7168.0)
REACH = 4
EDGE = 8
ROWS = 8
SPAN = 8

SMEM = pl.BlockSpec(memory_space=pltpu.SMEM)
VMEM = pl.BlockSpec(memory_space=pltpu.VMEM)
PARAMS = pltpu.CompilerParams(vmem_limit_bytes=36 * 1024 * 1024)


def entry_of(list_ref):
    return jnp.max(list_ref[0:1, 0:1].astype(jnp.float32)).astype(jnp.int32)


def combine(ahead, behind):
    total = None
    for order in range(1, 5):
        upper, lower = ahead(order), behind(order)
        if upper is None and lower is None:
            continue
        if lower is None:
            term = upper
        elif upper is None:
            term = -lower
        else:
            term = upper - lower
        if order > 1:
            term = (COEF[order - 1] / COEF[0]) * term
        total = term if total is None else total + term
    return total


def band(first, depth):
    source = lax.broadcasted_iota(jnp.int32, (depth, depth), 0)
    target = lax.broadcasted_iota(jnp.int32, (depth, depth), 1)
    total = jnp.zeros((depth, depth), jnp.float32)
    for order in range(1, 5):
        weight = COEF[order - 1] / COEF[0]
        total = total + jnp.where(source == target + (first + order - 1), weight, 0.0)
        total = total - jnp.where(source == target + (first - order), weight, 0.0)
    return jnp.concatenate(halves(total), axis=1)


def halves(values):
    high = values.astype(jnp.bfloat16)
    return high, (values - high.astype(jnp.float32)).astype(jnp.bfloat16)


def along_z(values, matrix):
    xs, ys, zs = values.shape
    pair = jnp.concatenate(halves(values.reshape(xs * ys, zs)), axis=1)
    parts = jnp.dot(pair, matrix, preferred_element_type=jnp.float32)
    return (parts[:, :zs] + parts[:, zs:]).reshape(xs, ys, zs)


def blocks(xs, ys, body):
    if xs <= SPAN:
        for y0 in range(0, ys, ROWS):
            body(0, xs, y0)
        return

    def span(index, _):
        for y0 in range(0, ys, ROWS):
            body(index * SPAN, SPAN, y0)
        return 0

    lax.fori_loop(0, xs // SPAN, span, 0)


def window(xs, x0, load):
    kept = {}

    def at(offset):
        if xs <= SPAN and not 0 <= offset < xs:
            return None
        if offset not in kept:
            kept[offset] = load(x0 + offset)
        return kept[offset]

    return at


def slopes(xs, p, x0, y0, plane, offset):
    centre = plane(offset)
    here = x0 + offset + REACH
    return (
        combine(lambda k: plane(offset + k), lambda k: plane(offset + 1 - k)),
        combine(
            lambda k: p[here, pl.ds(EDGE + y0 + k, ROWS)],
            lambda k: centre if k == 1 else p[here, pl.ds(EDGE + y0 + 1 - k, ROWS)],
        ),
    )


def prepare_kernel(
    steps, fwd, adj, src, wave, rec, res, _piece,
    fwd_slope, adj_slope, fwd_source, adj_source, ahead, behind, *fields,
):
    xs, ys, zs = fwd_slope.shape[1:]
    for ref, first in ((ahead, 1), (behind, 0)):
        one = band(first, zs)
        ref[:zs] = one
        ref[zs:] = one

    def clear(ref):
        ref[...] = jnp.zeros(ref.shape, jnp.float32)

    for state, (p, v0, v1, v2), slope in (
        (fwd, fields[:4], fwd_slope),
        (adj, fields[4:], adj_slope),
    ):
        for ref in (p, v0):
            clear(ref.at[:REACH])
            clear(ref.at[REACH + xs :])
        for ref in (p.at[pl.ds(REACH, xs)], v1):
            clear(ref.at[:, :EDGE])
            clear(ref.at[:, EDGE + ys :])
        for x in range(xs):
            p[REACH + x, EDGE : EDGE + ys] = state[0, 0, x].astype(jnp.float32)
            v0[REACH + x] = state[0, 1, x].astype(jnp.float32)
            v1[x, EDGE : EDGE + ys] = state[0, 2, x].astype(jnp.float32)
            v2[x] = state[0, 3, x].astype(jnp.float32)

        def block(x0, count, y0, p=p, slope=slope):
            plane = window(xs, x0, lambda x: p[REACH + x, pl.ds(EDGE + y0, ROWS)])
            for offset in range(count):
                for d, values in enumerate(slopes(xs, p, x0, y0, plane, offset)):
                    slope[d, x0 + offset, pl.ds(y0, ROWS)] = values

        blocks(xs, ys, block)
        slope[2] = along_z(p[REACH : REACH + xs, EDGE : EDGE + ys], ahead[...])

    row = lax.broadcasted_iota(jnp.int32, (ys, zs), 0)
    lane = lax.broadcasted_iota(jnp.int32, (ys, zs), 1)
    src_mark = (row == src[0, 1]) & (lane == src[0, 2])
    for x in range(xs):
        rec_mark = (row == rec[0, 0, x]) & (lane == rec[0, 1, x])
        for step in range(steps):
            amplitude = jnp.where(x == src[0, 0], wave[0, step], 0.0)
            fwd_source[step, x] = jnp.where(src_mark, amplitude, 0.0)
            adj_source[step, x] = jnp.where(rec_mark, res[0, step, x], 0.0)


def near_kernel(speed, density, aperture, near_speed, near_density, entry):
    near_speed[...] = speed[...]
    near_density[...] = density[...]
    entry[...] = jnp.full(entry.shape, entry_of(aperture), jnp.int32)


def pick_kernel(chips, near_speed, near_density, far_speed, far_density, *refs):
    stripes = 2 * chips
    lists, outs = refs[:stripes], refs[stripes:]
    held = near_speed.shape[0]
    me = lax.axis_index("tile")
    residue, half = lax.rem(me, stripes), lax.div(me, stripes)
    for hop in range(stripes):
        entry = entry_of(lists[hop])
        corner, column = lax.div(entry, held), lax.rem(entry, held)
        here = (residue >= corner) == (half == 0)
        piece = outs[hop]

        @pl.when(here)
        def _():
            piece[0] = near_speed[column]
            piece[1] = near_density[column]

        @pl.when(jnp.logical_not(here))
        def _():
            piece[0] = far_speed[column]
            piece[1] = far_density[column]


def wave_kernel(chips, steps, held, *refs):
    stripes = 2 * chips
    pieces, refs = refs[:stripes], refs[stripes:]
    fwd_slope, adj_slope, fwd_source, adj_source, ahead, behind, entry_ref = refs[:7]
    kept, traded, p, v0, v1, v2, q, w0, w1, w2 = refs[15:25]
    bulk, buoy, dp, dv, bulk_img, buoy_img, across_z, flat = refs[25:]
    tile_x, tile_y = pieces[0].shape[1:3]
    xs, ys, zs = bulk.shape
    residue = lax.rem(lax.axis_index("tile"), stripes)
    entry = entry_of(entry_ref)
    corner = lax.div(entry, held)

    def place_of(hop):
        return lax.rem((residue ^ hop) - corner + stripes, stripes) * tile_x

    for hop in range(stripes):
        cells = pl.ds(place_of(hop), tile_x)
        speed, density = pieces[hop][0], pieces[hop][1]
        bulk[cells] = COEF[0] * (density * speed * speed)
        buoy[cells] = COEF[0] / density

    def push(fields, first, note):
        p, v0, v1, v2 = fields
        if first is None:
            across_z[...] = along_z(p[REACH : REACH + xs, EDGE : EDGE + ys], ahead[...])

        def block(x0, count, y0):
            rows, inner = pl.ds(y0, ROWS), pl.ds(EDGE + y0, ROWS)
            plane = window(xs, x0, lambda x: p[REACH + x, inner])
            for offset in range(count):
                x = x0 + offset
                if first is None:
                    two = slopes(xs, p, x0, y0, plane, offset)
                else:
                    two = (first[0, x, rows], first[1, x, rows])
                light = buoy[x, rows]
                changes = (light * two[0], light * two[1])
                moved = (v0[REACH + x, rows] + changes[0], v1[x, inner] + changes[1])
                v0[REACH + x, rows] = moved[0]
                v1[x, inner] = moved[1]
                note(0, x, rows, changes, moved)

        def block_z(x0, count, y0):
            rows = pl.ds(y0, ROWS)
            for x in range(count):
                x = x0 + x
                slope = across_z[x, rows] if first is None else first[2, x, rows]
                change = buoy[x, rows] * slope
                moved = v2[x, rows] + change
                v2[x, rows] = moved
                note(2, x, rows, (change,), (moved,))

        blocks(xs, ys, block)
        blocks(xs, ys, block_z)

    def spread(fields, source, step, note):
        p, v0, v1, v2 = fields
        across_z[...] = along_z(v2[...], behind[...])

        def block(x0, count, y0):
            rows = pl.ds(y0, ROWS)
            plane = window(xs, x0, lambda x: v0[REACH + x, rows])
            for offset in range(count):
                x = x0 + offset
                along_x = combine(lambda k: plane(offset + k - 1), lambda k: plane(offset - k))
                along_y = combine(
                    lambda k: v1[x, pl.ds(EDGE + y0 + k - 1, ROWS)],
                    lambda k: v1[x, pl.ds(EDGE + y0 - k, ROWS)],
                )
                flat[x, rows] = along_x + along_y

        def block_z(x0, count, y0):
            rows, inner = pl.ds(y0, ROWS), pl.ds(EDGE + y0, ROWS)
            for x in range(count):
                x = x0 + x
                change = bulk[x, rows] * (flat[x, rows] + across_z[x, rows])
                change = change + source[step, x, rows]
                moved = p[REACH + x, inner] + change
                p[REACH + x, inner] = moved
                note(x, rows, change, moved)

        blocks(xs, ys, block)
        blocks(xs, ys, block_z)

    fields = (p, v0, v1, v2)
    for step in range(steps):

        def keep_dv(first, x, rows, changes, moved, step=step):
            for d, change in enumerate(changes, first):
                dv[step, d, x, rows] = change

        def keep_dp(x, rows, change, moved, step=step):
            dp[step, x, rows] = change

        push(fields, fwd_slope if step == 0 else None, keep_dv)
        spread(fields, fwd_source, step, keep_dp)

    fields = (q, w0, w1, w2)
    for step in reversed(range(steps)):
        last = step == steps - 1

        def add_buoy(first, x, rows, changes, moved, step=step, last=last):
            image = None if last and first == 0 else buoy_img[x, rows]
            for d, values in enumerate(moved, first):
                product = dv[step, d, x, rows] * values
                image = product if image is None else image + product
            buoy_img[x, rows] = image

        def add_bulk(x, rows, change, moved, step=step, last=last):
            image = dp[step, x, rows] * moved
            bulk_img[x, rows] = image if last else bulk_img[x, rows] + image

        push(fields, adj_slope if last else None, add_buoy)
        spread(fields, adj_source, step, add_bulk)

    tile_rows = tile_x * tile_y
    for chip in range(chips):
        for ref, hop in ((kept, 2 * chip), (traded, 2 * chip + 1)):
            cells = pl.ds(place_of(hop), tile_x)
            ref[chip, :tile_rows] = bulk_img[cells].reshape(tile_rows, zs)
            ref[chip, tile_rows : 2 * tile_rows] = buoy_img[cells].reshape(tile_rows, zs)
            ref[chip, 2 * tile_rows :] = jnp.full((8, zs), entry).astype(jnp.float32)


def return_order(chips):
    even = [chips] + list(range(1, chips)) + list(range(chips + 1, 2 * chips))
    return list(zip(even, reversed(even)))


def merge_kernel(chips, kept, came, *outs):
    rows = kept.shape[1] - 8
    odd = lax.rem(lax.axis_index("tile"), 2) == 1
    for out, (even_hop, odd_hop) in zip(outs, [(0, 0)] + return_order(chips)):
        chip = jnp.where(odd, odd_hop % chips, even_hop % chips)
        for shot, source in enumerate((kept, came)):
            out[shot * rows : (shot + 1) * rows] = source[chip, :rows]
            first = 2 * rows + 4 * shot
            out[first : first + 4] = source[chip, rows : rows + 4]


def add_kernel(chips, groups, held, *refs):
    came, parts, total = refs[: 2 * chips], refs[2 * chips : 2 * chips + groups], refs[-1]
    stripes = 2 * chips
    me, group = lax.axis_index("tile"), lax.axis_index("grp")
    tile_rows = total.shape[1] // (held + 1)
    part = parts[0].shape[1]
    total[...] = jnp.zeros_like(total)
    for pair in came:
        for shot in range(2):
            first = 4 * tile_rows + 4 * shot
            entry = jnp.max(pair[first : first + 4]).astype(jnp.int32)
            corner, column = lax.div(entry, held), lax.rem(entry, held)
            mine = (corner <= me) & (me < corner + stripes)
            slot = jnp.where(mine, column, held)
            rows = pl.ds(pl.multiple_of(slot * tile_rows, tile_rows), tile_rows)
            for field in range(2):
                first = (2 * shot + field) * tile_rows
                total[field, rows] = total[field, rows] + pair[first : first + tile_rows]
    for index, hop in enumerate([0] + far_first(groups)):
        first = pl.multiple_of((group ^ hop) * part, part)
        for field in range(2):
            parts[index][field] = total[field, pl.ds(first, part)]


def far_first(groups):
    return list(range(groups - 1, 0, -1))


def grads_kernel(scale, groups, *refs):
    parts, speed_ref, density_ref, grads = refs[:groups], *refs[groups:]
    part = parts[0].shape[1]
    rows = pl.ds(pl.multiple_of(lax.axis_index("grp") * part, part), part)
    speed, density = speed_ref[rows], density_ref[rows]
    bulk_sum, buoy_sum = parts[0][0], parts[0][1]
    for other in parts[1:]:
        bulk_sum = bulk_sum + other[0]
        buoy_sum = buoy_sum + other[1]
    grads[0] = scale * (bulk_sum * (2.0 * density * speed))
    grads[1] = scale * (bulk_sum * (speed * speed) - buoy_sum / (density * density))


def per_device(speed, density, fwd_state, adj_state, aperture, src_pos, wavelet, rec_pos, residual):
    owners = lax.axis_size("tile")
    groups = lax.axis_size("grp")
    my_group = lax.axis_index("grp")
    held, tile_x, tile_y, depth = speed.shape
    stripes = aperture.shape[1]
    chips = stripes // 2
    steps = wavelet.shape[1]
    xs = stripes * tile_x
    f32 = jnp.float32
    cells = (xs, tile_y, depth)

    def shape(*dims):
        return jax.ShapeDtypeStruct(dims, f32)

    def across(values, hop):
        return lax.ppermute(values, "tile", [(t, t ^ hop) for t in range(owners)])

    far_speed = across(speed, stripes)
    far_density = across(density, stripes)
    lists = {hop: across(aperture, hop) for hop in range(stripes - 1, 0, -1)}
    four = [
        (xs + 2 * REACH, tile_y + 2 * EDGE, depth),
        (xs + 2 * REACH, tile_y, depth),
        (xs, tile_y + 2 * EDGE, depth),
        cells,
    ]
    near_speed, near_density, entry = pl.pallas_call(
        near_kernel,
        out_shape=[
            shape(*speed.shape),
            shape(*speed.shape),
            jax.ShapeDtypeStruct((8, depth), jnp.int32),
        ],
        in_specs=[VMEM] * 3,
        out_specs=[VMEM] * 3,
        compiler_params=PARAMS,
        cost_estimate=pl.CostEstimate(flops=4_000_000, bytes_accessed=6_000_000, transcendentals=0),
        name="hold_near_tiles",
    )(speed, density, aperture)
    pieces = pl.pallas_call(
        functools.partial(pick_kernel, chips),
        out_shape=[shape(2, tile_x, tile_y, depth)] * stripes,
        in_specs=[VMEM] * (4 + stripes),
        out_specs=[VMEM] * stripes,
        compiler_params=PARAMS,
        name="pick_tiles",
    )(near_speed, near_density, far_speed, far_density, entry, *[lists[h] for h in range(1, stripes)])
    moved = {hop: across(pieces[hop], hop) for hop in range(stripes - 1, 0, -1)}

    prepared = pl.pallas_call(
        functools.partial(prepare_kernel, steps),
        out_shape=[shape(3, *cells)] * 2
        + [shape(steps, *cells)] * 2
        + [jax.ShapeDtypeStruct((2 * depth, 2 * depth), jnp.bfloat16)] * 2
        + [shape(*dims) for dims in four + four],
        in_specs=[VMEM] * 2 + [SMEM] * 4 + [VMEM],
        out_specs=[VMEM] * 14,
        compiler_params=PARAMS,
        cost_estimate=pl.CostEstimate(flops=4_000_000, bytes_accessed=6_000_000, transcendentals=0),
        name="prepare",
    )(fwd_state, adj_state, src_pos, wavelet, jnp.swapaxes(rec_pos, 1, 2), residual, pieces[0])
    prepared, fields = prepared[:6], prepared[6:]
    pieces = [pieces[0]] + [moved[hop] for hop in range(1, stripes)]

    tile_rows = tile_x * tile_y
    sent = shape(chips, 2 * tile_rows + 8, depth)
    kept, traded, *_ = pl.pallas_call(
        functools.partial(wave_kernel, chips, steps, held),
        out_shape=[sent, sent] + [shape(*dims) for dims in four + four],
        in_specs=[VMEM] * (stripes + 15),
        out_specs=[VMEM] * 10,
        scratch_shapes=[
            pltpu.VMEM(cells, f32),
            pltpu.VMEM(cells, f32),
            pltpu.VMEM((steps,) + cells, f32),
            pltpu.VMEM((steps, 3) + cells, f32),
        ]
        + [pltpu.VMEM(cells, f32)] * 4
        + [
        ],
        input_output_aliases={stripes + 7 + index: 2 + index for index in range(8)},
        compiler_params=PARAMS,
        name="replay_and_adjoint",
    )(*pieces, *prepared, entry, *fields)

    both = shape(4 * tile_rows + 8, depth)
    stacks = pl.pallas_call(
        functools.partial(merge_kernel, chips),
        out_shape=[both] * stripes,
        in_specs=[VMEM] * 2,
        out_specs=[VMEM] * stripes,
        compiler_params=PARAMS,
        name="merge_pair",
    )(kept, across(traded, 1))
    came = [
        lax.ppermute(values, "tile", [(t, t ^ (2 * hops[t % 2])) for t in range(owners)])
        for values, hops in zip(stacks[1:], return_order(chips))
    ]
    came = came[-1:] + came[:-1]

    rows = held * tile_rows
    part = rows // groups
    part_shape = shape(2, part, depth)
    parts = pl.pallas_call(
        functools.partial(add_kernel, chips, groups, held),
        out_shape=[part_shape] * groups,
        in_specs=[VMEM] * stripes,
        out_specs=[VMEM] * groups,
        scratch_shapes=[pltpu.VMEM((2, rows + tile_rows, depth), f32)],
        compiler_params=PARAMS,
        name="add_stripes",
    )(stacks[0], *came)

    def along(values, hop):
        return lax.ppermute(values, "grp", [(g, g ^ hop) for g in range(groups)])

    parts = [parts[0]] + [along(values, hop) for values, hop in zip(parts[1:], far_first(groups))]
    grads = pl.pallas_call(
        functools.partial(grads_kernel, 1.0 / math.sqrt(groups * owners), groups),
        out_shape=part_shape,
        in_specs=[VMEM] * (groups + 2),
        out_specs=VMEM,
        compiler_params=PARAMS,
        name="gradients",
    )(*parts, near_speed.reshape(rows, depth), near_density.reshape(rows, depth))

    whole = jnp.zeros((2, groups, part, depth), f32)
    for hop in range(groups):
        values = grads
        if hop:
            values = lax.ppermute(grads, "grp", [(g, (g + hop) % groups) for g in range(groups)])
        place = lax.rem(my_group - hop + groups, groups)
        whole = lax.dynamic_update_slice_in_dim(whole, values[:, None], place, axis=1)
    return (whole[0].reshape(speed.shape), whole[1].reshape(speed.shape))


def solution(mesh):
    return jax.shard_map(
        per_device,
        mesh=mesh,
        in_specs=(
            P("tile", None, None, None),
            P("tile", None, None, None),
            P(("grp", "tile"), None, None, None, None),
            P(("grp", "tile"), None, None, None, None),
            P(("grp", "tile"), None),
            P(("grp", "tile"), None),
            P(("grp", "tile"), None),
            P(("grp", "tile"), None, None),
            P(("grp", "tile"), None, None),
        ),
        out_specs=(P("tile", None, None, None), P("tile", None, None, None)),
        check_vma=False,
    )
```

profile of v0, /device:TPU:0, one launch (start us, length us, event | category | flops | bytes accessed | tf_op | source)
XLA Modules:
  0.0 47.0 jit_solution(1952673741111824847)
XLA Ops:
  0.6 3.0 %collective-permute-start = (f32[4,2,32,128]{3,2,1,0:T(8,128)}, f32[4,2,32,128]{3,2,1,0:T(8,128)S(1)}, u32[]{:S(2)}, u32[]{:S(2)}) collective-permute-start(f32[4,2,32,128]{3,2,1,0:T(8,128)} %speed.1), channel_id=1, source_target_pairs={{0,4},{1,5},{2,6},{3,7},{4,0},{5,1},{6,2},{7,3},{8,12},{9,13},{10,... | collective-permute-start | bytes 393224 | tf_op jit(solution)/shard_map/ppermute | solution.py:381
  3.7 0.1 collective-permute-start.1
  3.7 0.0 collective-permute-start.2
  3.7 1.9 %collective-permute-start.3 = (s32[1,4]{1,0:T(1,128)}, s32[1,4]{1,0:T(1,128)S(1)}, u32[]{:S(2)}, u32[]{:S(2)}) collective-permute-start(s32[1,4]{1,0:T(1,128)} %aperture.1), channel_id=1, source_target_pairs={{0,2},{1,3},{2,0},{3,1},{4,6},{5,7},{6,4},{7,5},{8,10},{9,11},{10,... | collective-permute-start | bytes 56 | tf_op jit(solution)/shard_map/ppermute | solution.py:381
  5.7 0.2 collective-permute-start.4
  5.8 0.0 copy-start.2
  5.8 0.9 %copy-done.2 = f32[4,2,32,128]{3,2,1,0:T(8,128)S(1)} copy-done((f32[4,2,32,128]{3,2,1,0:T(8,128)S(1)}, f32[4,2,32,128]{3,2,1,0:T(8,128)}, u32[]{:S(2)}) %copy-start.2) | copy-done | bytes 131096
  6.7 0.0 copy-start.3
  6.7 0.9 %copy-done.3 = f32[4,2,32,128]{3,2,1,0:T(8,128)S(1)} copy-done((f32[4,2,32,128]{3,2,1,0:T(8,128)S(1)}, f32[4,2,32,128]{3,2,1,0:T(8,128)}, u32[]{:S(2)}) %copy-start.3) | copy-done | bytes 131096
  7.6 0.0 copy-start.6
  7.6 0.7 %copy-done.6 = s32[1,4]{1,0:T(1,128)S(1)} copy-done((s32[1,4]{1,0:T(1,128)S(1)}, s32[1,4]{1,0:T(1,128)}, u32[]{:S(2)}) %copy-start.6) | copy-done | bytes 40
  8.3 0.1 hold_near_tiles.1
  8.4 0.0 collective-permute-done.2.refs_1_
  8.4 0.0 collective-permute-done.3.refs_2_
  8.4 0.4 collective-permute-done.4.refs_3_
  8.8 0.0 collective-permute-done.far_speed
  8.8 1.4 %collective-permute-done.1.far_density = f32[4,2,32,128]{3,2,1,0:T(8,128)S(1)} collective-permute-done((f32[4,2,32,128]{3,2,1,0:T(8,128)}, f32[4,2,32,128]{3,2,1,0:T(8,128)S(1)}, u32[]{:S(2)}, u32[]{:S(2)}) %collective-permute-start.1) | collective-permute-done | bytes 131104 | tf_op jit(solution)/shard_map/ppermute | solution.py:381
  10.2 0.0 copy-start
  10.2 0.0 copy-start.1
  10.2 0.0 copy-start.8
  10.2 0.2 pick_tiles.1
  10.4 0.1 collective-permute-start.5
  10.5 1.8 %collective-permute-start.6 = (f32[2,2,32,128]{3,2,1,0:T(8,128)S(1)}, f32[2,2,32,128]{3,2,1,0:T(8,128)S(1)}, u32[]{:S(2)}, u32[]{:S(2)}) collective-permute-start(f32[2,2,32,128]{3,2,1,0:T(8,128)S(1)} %get-tuple-element.38), channel_id=1, source_target_pairs={{0,2},{1,3},{2,0},{3,1},{4,6},{5,7},{6,4},{7,5},{8,10},{9,11},{10,... | collective-permute-start | bytes 196616 | tf_op jit(solution)/shard_map/ppermute | solution.py:381
  12.3 0.0 copy-start.4
  12.3 0.1 collective-permute-start.7
  12.3 0.0 copy-start.5
  12.3 0.0 copy-start.7
  12.3 0.0 copy-done
  12.4 0.0 copy-done.1
  12.4 0.0 copy-done.8
  12.4 0.6 %copy-done.4 = f32[1,4,8]{2,1,0:T(4,128)S(1)} copy-done((f32[1,4,8]{2,1,0:T(4,128)S(1)}, f32[1,4,8]{2,1,0:T(4,128)}, u32[]{:S(2)}) %copy-start.4) | copy-done | bytes 152
  12.9 0.1 copy-done.5
  13.0 0.0 copy-done.7
  13.0 1.3 %prepare.1 = (f32[3,8,32,128]{3,2,1,0:T(8,128)S(1)}, f32[3,8,32,128]{3,2,1,0:T(8,128)S(1)}, f32[4,8,32,128]{3,2,1,0:T(8,128)S(1)}, f32[4,8,32,128]{3,2,1,0:T(8,1...) custom-call(bf16[1,4,8,32,128]{4,3,2,1,0:T(8,128)(2,1)S(1)} %copy-do, ...), custom_call_target="tpu_custom_call" | custom-call | flops 4000000 | bytes 6000000 | tf_op jit(solution)/shard_map/prepare/pallas_call | solution.py:415
  14.3 0.0 collective-permute-done.5.refs_1_
  14.3 0.7 %collective-permute-done.6.refs_2_ = f32[2,2,32,128]{3,2,1,0:T(8,128)S(1)} collective-permute-done((f32[2,2,32,128]{3,2,1,0:T(8,128)S(1)}, f32[2,2,32,128]{3,2,1,0:T(8,128)S(1)}, u32[]{:S(2)}, u32[]{:S(2)}) %collective-permute-start.6) | collective-permute-done | bytes 65568 | tf_op jit(solution)/shard_map/ppermute | solution.py:381
  15.0 1.3 %collective-permute-done.7.refs_3_ = f32[2,2,32,128]{3,2,1,0:T(8,128)S(1)} collective-permute-done((f32[2,2,32,128]{3,2,1,0:T(8,128)S(1)}, f32[2,2,32,128]{3,2,1,0:T(8,128)S(1)}, u32[]{:S(2)}, u32[]{:S(2)}) %collective-permute-start.7) | collective-permute-done | bytes 65568 | tf_op jit(solution)/shard_map/ppermute | solution.py:381
  16.3 2.4 %replay_and_adjoint.1 = (f32[2,136,128]{2,1,0:T(8,128)S(1)}, f32[2,136,128]{2,1,0:T(8,128)S(1)}, f32[16,48,128]{2,1,0:T(8,128)S(1)}, f32[16,32,128]{2,1,0:T(8,12...) custom-call(f32[2,2,32,128]{3,2,1,0:T(8,128)S(1)} %get-tuple-element, ...), custom_call_target="tpu_custom_call", output_to_operand_aliasing={{2}: (11, {}), {3}: (12, {}), {4}: (13, {}), {5}: (14, {}),... | custom-call | tf_op jit(solution)/shard_map/replay_and_adjoint/pallas_call | solution.py:432
  18.7 0.2 collective-permute-start.8
  18.9 1.2 %collective-permute-done.8.came = f32[2,136,128]{2,1,0:T(8,128)S(1)} collective-permute-done((f32[2,136,128]{2,1,0:T(8,128)S(1)}, f32[2,136,128]{2,1,0:T(8,128)S(1)}, u32[]{:S(2)}, u32[]{:S(2)}) %collective-permute-start.8) | collective-permute-done | bytes 139296 | tf_op jit(solution)/shard_map/ppermute | solution.py:381
  20.1 1.6 %collective-permute-start.10 = (f32[264,128]{1,0:T(8,128)S(1)}, f32[264,128]{1,0:T(8,128)S(1)}, u32[]{:S(2)}, u32[]{:S(2)}) collective-permute-start(f32[264,128]{1,0:T(8,128)S(1)} %get-tuple-element.58), channel_id=1, source_target_pairs={{0,4},{1,7},{2,6},{3,5},{4,0},{5,3},{6,2},{7,1},{8,12},{9,15},{10,... | collective-permute-start | bytes 405512 | tf_op jit(solution)/shard_map/ppermute | solution.py:461
  21.7 1.3 %collective-permute-start.11 = (f32[264,128]{1,0:T(8,128)S(1)}, f32[264,128]{1,0:T(8,128)S(1)}, u32[]{:S(2)}, u32[]{:S(2)}) collective-permute-start(f32[264,128]{1,0:T(8,128)S(1)} %get-tuple-element.59), channel_id=1, source_target_pairs={{0,2},{1,3},{2,0},{3,1},{4,6},{5,7},{6,4},{7,5},{8,10},{9,11},{10,... | collective-permute-start | bytes 405512 | tf_op jit(solution)/shard_map/ppermute | solution.py:461
  23.1 0.6 %collective-permute-start.9 = (f32[264,128]{1,0:T(8,128)S(1)}, f32[264,128]{1,0:T(8,128)S(1)}, u32[]{:S(2)}, u32[]{:S(2)}) collective-permute-start(f32[264,128]{1,0:T(8,128)S(1)} %get-tuple-element.57), channel_id=1, source_target_pairs={{0,6},{1,5},{2,4},{3,7},{4,2},{5,1},{6,0},{7,3},{8,14},{9,13},{10,... | collective-permute-start | bytes 405512 | tf_op jit(solution)/shard_map/ppermute | solution.py:461
  23.7 4.2 %collective-permute-done.10.refs_2_ = f32[264,128]{1,0:T(8,128)S(1)} collective-permute-done((f32[264,128]{1,0:T(8,128)S(1)}, f32[264,128]{1,0:T(8,128)S(1)}, u32[]{:S(2)}, u32[]{:S(2)}) %collective-permute-start.10) | collective-permute-done | bytes 135200 | tf_op jit(solution)/shard_map/ppermute | solution.py:461
  27.9 0.3 collective-permute-done.11.refs_3_
  28.2 1.5 %collective-permute-done.9.refs_1_ = f32[264,128]{1,0:T(8,128)S(1)} collective-permute-done((f32[264,128]{1,0:T(8,128)S(1)}, f32[264,128]{1,0:T(8,128)S(1)}, u32[]{:S(2)}, u32[]{:S(2)}) %collective-permute-start.9) | collective-permute-done | bytes 135200 | tf_op jit(solution)/shard_map/ppermute | solution.py:461
  29.7 0.2 add_stripes.1
  29.9 3.7 %collective-permute-start.12 = (f32[2,64,128]{2,1,0:T(8,128)S(1)}, f32[2,64,128]{2,1,0:T(8,128)S(1)}, u32[]{:S(2)}, u32[]{:S(2)}) collective-permute-start(f32[2,64,128]{2,1,0:T(8,128)S(1)} %get-tuple-element.61), channel_id=1, source_target_pairs={{0,24},{8,16},{16,8},{24,0},{1,25},{9,17},{17,9},{25,1},{2,26},{10... | collective-permute-start | bytes 196616 | tf_op jit(solution)/shard_map/ppermute | solution.py:480
  33.6 0.0 collective-permute-start.13
  33.6 0.8 %collective-permute-start.14 = (f32[2,64,128]{2,1,0:T(8,128)S(1)}, f32[2,64,128]{2,1,0:T(8,128)S(1)}, u32[]{:S(2)}, u32[]{:S(2)}) collective-permute-start(f32[2,64,128]{2,1,0:T(8,128)S(1)} %get-tuple-element.63), channel_id=1, source_target_pairs={{0,8},{8,0},{16,24},{24,16},{1,9},{9,1},{17,25},{25,17},{2,10},{10... | collective-permute-start | bytes 196616 | tf_op jit(solution)/shard_map/ppermute | solution.py:480
  34.4 1.7 %collective-permute-done.12.refs_1_ = f32[2,64,128]{2,1,0:T(8,128)S(1)} collective-permute-done((f32[2,64,128]{2,1,0:T(8,128)S(1)}, f32[2,64,128]{2,1,0:T(8,128)S(1)}, u32[]{:S(2)}, u32[]{:S(2)}) %collective-permute-start.12) | collective-permute-done | bytes 65568 | tf_op jit(solution)/shard_map/ppermute | solution.py:480
  36.1 2.8 %collective-permute-done.13.refs_2_ = f32[2,64,128]{2,1,0:T(8,128)S(1)} collective-permute-done((f32[2,64,128]{2,1,0:T(8,128)S(1)}, f32[2,64,128]{2,1,0:T(8,128)S(1)}, u32[]{:S(2)}, u32[]{:S(2)}) %collective-permute-start.13) | collective-permute-done | bytes 65568 | tf_op jit(solution)/shard_map/ppermute | solution.py:480
  38.9 0.0 collective-permute-done.14.refs_3_
  38.9 0.5 collective-permute-start.15
  39.4 2.3 %collective-permute-start.16 = (f32[2,64,128]{2,1,0:T(8,128)S(1)}, f32[2,64,128]{2,1,0:T(8,128)S(1)}, u32[]{:S(2)}, u32[]{:S(2)}) collective-permute-start(f32[2,64,128]{2,1,0:T(8,128)S(1)} %gradients.1), channel_id=1, source_target_pairs={{0,16},{8,24},{16,0},{24,8},{1,17},{9,25},{17,1},{25,9},{2,18},{10... | collective-permute-start | bytes 196616 | tf_op jit(solution)/shard_map/ppermute | solution.py:496
  41.7 2.1 %collective-permute-start.17 = (f32[2,64,128]{2,1,0:T(8,128)S(1)}, f32[2,64,128]{2,1,0:T(8,128)S(1)}, u32[]{:S(2)}, u32[]{:S(2)}) collective-permute-start(f32[2,64,128]{2,1,0:T(8,128)S(1)} %gradients.1), channel_id=1, source_target_pairs={{0,24},{8,0},{16,8},{24,16},{1,25},{9,1},{17,9},{25,17},{2,26},{10... | collective-permute-start | bytes 196616 | tf_op jit(solution)/shard_map/ppermute | solution.py:496
  43.8 1.3 %collective-permute-done.15 = f32[2,64,128]{2,1,0:T(8,128)S(1)} collective-permute-done((f32[2,64,128]{2,1,0:T(8,128)S(1)}, f32[2,64,128]{2,1,0:T(8,128)S(1)}, u32[]{:S(2)}, u32[]{:S(2)}) %collective-permute-start.15) | collective-permute-done | bytes 65568 | tf_op jit(solution)/shard_map/ppermute | solution.py:496
  45.2 1.1 %collective-permute-done.16 = f32[2,64,128]{2,1,0:T(8,128)S(1)} collective-permute-done((f32[2,64,128]{2,1,0:T(8,128)S(1)}, f32[2,64,128]{2,1,0:T(8,128)S(1)}, u32[]{:S(2)}, u32[]{:S(2)}) %collective-permute-start.16) | collective-permute-done | bytes 65568 | tf_op jit(solution)/shard_map/ppermute | solution.py:496
  46.3 0.0 collective-permute-done.17
  46.3 0.7 %fusion = (f32[1,4,64,128]{3,2,1,0:T(8,128)}, f32[1,4,64,128]{3,2,1,0:T(8,128)}) fusion(f32[2,4,64,128]{3,2,1,0:T(8,128)S(1)} %bitcast_dynamic-update-slice_fusion), kind=kLoop, calls=%fused_computation.4 | loop fusion | bytes 524288 | tf_op jit(solution)/shard_map/slice | solution.py:499
  (8 shorter events, 0.1 us)
Async XLA Ops:
  0.6 8.1 %collective-permute-start = (f32[4,2,32,128]{3,2,1,0:T(8,128)}, f32[4,2,32,128]{3,2,1,0:T(8,128)S(1)}, u32[]{:S(2)}, u32[]{:S(2)}) collective-permute-start(f32[4,2,32,128]{3,2,1,0:T(8,128)} %speed.1), channel_id=1, source_target_pairs={{0,4},{1,5},{2,6},{3,7},{4,0},{5,1},{6,2},{7,3},{8,12},{9,13},{10,... | collective-permute-start | bytes 393224 | tf_op jit(solution)/shard_map/ppermute | solution.py:381
  3.7 6.5 %collective-permute-start.1 = (f32[4,2,32,128]{3,2,1,0:T(8,128)}, f32[4,2,32,128]{3,2,1,0:T(8,128)S(1)}, u32[]{:S(2)}, u32[]{:S(2)}) collective-permute-start(f32[4,2,32,128]{3,2,1,0:T(8,128)} %density.1), channel_id=1, source_target_pairs={{0,4},{1,5},{2,6},{3,7},{4,0},{5,1},{6,2},{7,3},{8,12},{9,13},{10,... | collective-permute-start | bytes 393224 | tf_op jit(solution)/shard_map/ppermute | solution.py:381
  3.7 4.6 %collective-permute-start.2 = (s32[1,4]{1,0:T(1,128)}, s32[1,4]{1,0:T(1,128)S(1)}, u32[]{:S(2)}, u32[]{:S(2)}) collective-permute-start(s32[1,4]{1,0:T(1,128)} %aperture.1), channel_id=1, source_target_pairs={{0,1},{1,0},{2,3},{3,2},{4,5},{5,4},{6,7},{7,6},{8,9},{9,8},{10,11... | collective-permute-start | bytes 56 | tf_op jit(solution)/shard_map/ppermute | solution.py:381
  3.7 4.6 %collective-permute-start.3 = (s32[1,4]{1,0:T(1,128)}, s32[1,4]{1,0:T(1,128)S(1)}, u32[]{:S(2)}, u32[]{:S(2)}) collective-permute-start(s32[1,4]{1,0:T(1,128)} %aperture.1), channel_id=1, source_target_pairs={{0,2},{1,3},{2,0},{3,1},{4,6},{5,7},{6,4},{7,5},{8,10},{9,11},{10,... | collective-permute-start | bytes 56 | tf_op jit(solution)/shard_map/ppermute | solution.py:381
  5.7 3.1 %collective-permute-start.4 = (s32[1,4]{1,0:T(1,128)}, s32[1,4]{1,0:T(1,128)S(1)}, u32[]{:S(2)}, u32[]{:S(2)}) collective-permute-start(s32[1,4]{1,0:T(1,128)} %aperture.1), channel_id=1, source_target_pairs={{0,3},{1,2},{2,1},{3,0},{4,7},{5,6},{6,5},{7,4},{8,11},{9,10},{10,... | collective-permute-start | bytes 56 | tf_op jit(solution)/shard_map/ppermute | solution.py:381
  5.8 0.9 %copy-start.2 = (f32[4,2,32,128]{3,2,1,0:T(8,128)S(1)}, f32[4,2,32,128]{3,2,1,0:T(8,128)}, u32[]{:S(2)}) copy-start(f32[4,2,32,128]{3,2,1,0:T(8,128)} %speed.1) | copy-start | bytes 393220
  6.7 0.9 %copy-start.3 = (f32[4,2,32,128]{3,2,1,0:T(8,128)S(1)}, f32[4,2,32,128]{3,2,1,0:T(8,128)}, u32[]{:S(2)}) copy-start(f32[4,2,32,128]{3,2,1,0:T(8,128)} %density.1) | copy-start | bytes 393220
  7.6 0.7 %copy-start.6 = (s32[1,4]{1,0:T(1,128)S(1)}, s32[1,4]{1,0:T(1,128)}, u32[]{:S(2)}) copy-start(s32[1,4]{1,0:T(1,128)} %aperture.1) | copy-start | bytes 52
  10.2 2.2 %copy-start = (bf16[1,4,8,32,128]{4,3,2,1,0:T(8,128)(2,1)S(1)}, bf16[1,4,8,32,128]{4,3,2,1,0:T(8,128)(2,1)}, u32[]{:S(2)}) copy-start(bf16[1,4,8,32,128]{4,3,2,1,0:T(8,128)(2,1)} %fwd.1) | copy-start | bytes 786436
  10.2 2.2 %copy-start.1 = (bf16[1,4,8,32,128]{4,3,2,1,0:T(8,128)(2,1)S(1)}, bf16[1,4,8,32,128]{4,3,2,1,0:T(8,128)(2,1)}, u32[]{:S(2)}) copy-start(bf16[1,4,8,32,128]{4,3,2,1,0:T(8,128)(2,1)} %adj.1) | copy-start | bytes 786436
  10.2 2.2 %copy-start.8 = (f32[1,4]{1,0:T(1,128)S(1)}, f32[1,4]{1,0:T(1,128)}, u32[]{:S(2)}) copy-start(f32[1,4]{1,0:T(1,128)} %wave.1) | copy-start | bytes 52
  10.4 3.9 %collective-permute-start.5 = (f32[2,2,32,128]{3,2,1,0:T(8,128)S(1)}, f32[2,2,32,128]{3,2,1,0:T(8,128)S(1)}, u32[]{:S(2)}, u32[]{:S(2)}) collective-permute-start(f32[2,2,32,128]{3,2,1,0:T(8,128)S(1)} %get-tuple-element.37), channel_id=1, source_target_pairs={{0,1},{1,0},{2,3},{3,2},{4,5},{5,4},{6,7},{7,6},{8,9},{9,8},{10,11... | collective-permute-start | bytes 196616 | tf_op jit(solution)/shard_map/ppermute | solution.py:381
  10.5 4.5 %collective-permute-start.6 = (f32[2,2,32,128]{3,2,1,0:T(8,128)S(1)}, f32[2,2,32,128]{3,2,1,0:T(8,128)S(1)}, u32[]{:S(2)}, u32[]{:S(2)}) collective-permute-start(f32[2,2,32,128]{3,2,1,0:T(8,128)S(1)} %get-tuple-element.38), channel_id=1, source_target_pairs={{0,2},{1,3},{2,0},{3,1},{4,6},{5,7},{6,4},{7,5},{8,10},{9,11},{10,... | collective-permute-start | bytes 196616 | tf_op jit(solution)/shard_map/ppermute | solution.py:381
  12.3 0.7 %copy-start.4 = (f32[1,4,8]{2,1,0:T(4,128)S(1)}, f32[1,4,8]{2,1,0:T(4,128)}, u32[]{:S(2)}) copy-start(f32[1,4,8]{2,1,0:T(4,128)} %res.1) | copy-start | bytes 388
  12.3 4.0 %collective-permute-start.7 = (f32[2,2,32,128]{3,2,1,0:T(8,128)S(1)}, f32[2,2,32,128]{3,2,1,0:T(8,128)S(1)}, u32[]{:S(2)}, u32[]{:S(2)}) collective-permute-start(f32[2,2,32,128]{3,2,1,0:T(8,128)S(1)} %get-tuple-element.39), channel_id=1, source_target_pairs={{0,3},{1,2},{2,1},{3,0},{4,7},{5,6},{6,5},{7,4},{8,11},{9,10},{10,... | collective-permute-start | bytes 196616 | tf_op jit(solution)/shard_map/ppermute | solution.py:381
  12.3 0.7 %copy-start.5 = (s32[1,8,2]{1,2,0:T(2,128)S(1)}, s32[1,8,2]{1,2,0:T(2,128)}, u32[]{:S(2)}) copy-start(s32[1,8,2]{1,2,0:T(2,128)} %param.16) | copy-start | bytes 196
  12.3 0.7 %copy-start.7 = (s32[1,3]{1,0:T(1,128)S(1)}, s32[1,3]{1,0:T(1,128)}, u32[]{:S(2)}) copy-start(s32[1,3]{1,0:T(1,128)} %src.1) | copy-start | bytes 40
  18.7 1.4 %collective-permute-start.8 = (f32[2,136,128]{2,1,0:T(8,128)S(1)}, f32[2,136,128]{2,1,0:T(8,128)S(1)}, u32[]{:S(2)}, u32[]{:S(2)}) collective-permute-start(f32[2,136,128]{2,1,0:T(8,128)S(1)} %get-tuple-element.55), channel_id=1, source_target_pairs={{0,1},{1,0},{2,3},{3,2},{4,5},{5,4},{6,7},{7,6},{8,9},{9,8},{10,11... | collective-permute-start | bytes 417800 | tf_op jit(solution)/shard_map/ppermute | solution.py:381
  20.1 7.8 %collective-permute-start.10 = (f32[264,128]{1,0:T(8,128)S(1)}, f32[264,128]{1,0:T(8,128)S(1)}, u32[]{:S(2)}, u32[]{:S(2)}) collective-permute-start(f32[264,128]{1,0:T(8,128)S(1)} %get-tuple-element.58), channel_id=1, source_target_pairs={{0,4},{1,7},{2,6},{3,5},{4,0},{5,3},{6,2},{7,1},{8,12},{9,15},{10,... | collective-permute-start | bytes 405512 | tf_op jit(solution)/shard_map/ppermute | solution.py:461
  21.7 6.5 %collective-permute-start.11 = (f32[264,128]{1,0:T(8,128)S(1)}, f32[264,128]{1,0:T(8,128)S(1)}, u32[]{:S(2)}, u32[]{:S(2)}) collective-permute-start(f32[264,128]{1,0:T(8,128)S(1)} %get-tuple-element.59), channel_id=1, source_target_pairs={{0,2},{1,3},{2,0},{3,1},{4,6},{5,7},{6,4},{7,5},{8,10},{9,11},{10,... | collective-permute-start | bytes 405512 | tf_op jit(solution)/shard_map/ppermute | solution.py:461
  23.1 6.6 %collective-permute-start.9 = (f32[264,128]{1,0:T(8,128)S(1)}, f32[264,128]{1,0:T(8,128)S(1)}, u32[]{:S(2)}, u32[]{:S(2)}) collective-permute-start(f32[264,128]{1,0:T(8,128)S(1)} %get-tuple-element.57), channel_id=1, source_target_pairs={{0,6},{1,5},{2,4},{3,7},{4,2},{5,1},{6,0},{7,3},{8,14},{9,13},{10,... | collective-permute-start | bytes 405512 | tf_op jit(solution)/shard_map/ppermute | solution.py:461
  29.9 6.2 %collective-permute-start.12 = (f32[2,64,128]{2,1,0:T(8,128)S(1)}, f32[2,64,128]{2,1,0:T(8,128)S(1)}, u32[]{:S(2)}, u32[]{:S(2)}) collective-permute-start(f32[2,64,128]{2,1,0:T(8,128)S(1)} %get-tuple-element.61), channel_id=1, source_target_pairs={{0,24},{8,16},{16,8},{24,0},{1,25},{9,17},{17,9},{25,1},{2,26},{10... | collective-permute-start | bytes 196616 | tf_op jit(solution)/shard_map/ppermute | solution.py:480
  33.6 5.3 %collective-permute-start.13 = (f32[2,64,128]{2,1,0:T(8,128)S(1)}, f32[2,64,128]{2,1,0:T(8,128)S(1)}, u32[]{:S(2)}, u32[]{:S(2)}) collective-permute-start(f32[2,64,128]{2,1,0:T(8,128)S(1)} %get-tuple-element.62), channel_id=1, source_target_pairs={{0,16},{8,24},{16,0},{24,8},{1,17},{9,25},{17,1},{25,9},{2,18},{10... | collective-permute-start | bytes 196616 | tf_op jit(solution)/shard_map/ppermute | solution.py:480
  33.6 5.3 %collective-permute-start.14 = (f32[2,64,128]{2,1,0:T(8,128)S(1)}, f32[2,64,128]{2,1,0:T(8,128)S(1)}, u32[]{:S(2)}, u32[]{:S(2)}) collective-permute-start(f32[2,64,128]{2,1,0:T(8,128)S(1)} %get-tuple-element.63), channel_id=1, source_target_pairs={{0,8},{8,0},{16,24},{24,16},{1,9},{9,1},{17,25},{25,17},{2,10},{10... | collective-permute-start | bytes 196616 | tf_op jit(solution)/shard_map/ppermute | solution.py:480
  38.9 6.2 %collective-permute-start.15 = (f32[2,64,128]{2,1,0:T(8,128)S(1)}, f32[2,64,128]{2,1,0:T(8,128)S(1)}, u32[]{:S(2)}, u32[]{:S(2)}) collective-permute-start(f32[2,64,128]{2,1,0:T(8,128)S(1)} %gradients.1), channel_id=1, source_target_pairs={{0,8},{8,16},{16,24},{24,0},{1,9},{9,17},{17,25},{25,1},{2,10},{10... | collective-permute-start | bytes 196616 | tf_op jit(solution)/shard_map/ppermute | solution.py:496
  39.4 6.9 %collective-permute-start.16 = (f32[2,64,128]{2,1,0:T(8,128)S(1)}, f32[2,64,128]{2,1,0:T(8,128)S(1)}, u32[]{:S(2)}, u32[]{:S(2)}) collective-permute-start(f32[2,64,128]{2,1,0:T(8,128)S(1)} %gradients.1), channel_id=1, source_target_pairs={{0,16},{8,24},{16,0},{24,8},{1,17},{9,25},{17,1},{25,9},{2,18},{10... | collective-permute-start | bytes 196616 | tf_op jit(solution)/shard_map/ppermute | solution.py:496
  41.7 4.6 %collective-permute-start.17 = (f32[2,64,128]{2,1,0:T(8,128)S(1)}, f32[2,64,128]{2,1,0:T(8,128)S(1)}, u32[]{:S(2)}, u32[]{:S(2)}) collective-permute-start(f32[2,64,128]{2,1,0:T(8,128)S(1)} %gradients.1), channel_id=1, source_target_pairs={{0,24},{8,0},{16,8},{24,16},{1,25},{9,1},{17,9},{25,17},{2,26},{10... | collective-permute-start | bytes 196616 | tf_op jit(solution)/shard_map/ppermute | solution.py:496
where the time goes:
time: 47.2 us; the launch traced here: 47 us
  starting transfers between devices  20.2 us (43%)
  waiting for transfers between devices  17.9 us (38%)
  Pallas kernels  4.17 us (9%)
  local copies, waits for them, and re-layouts  3.93 us (8%)
  between operations  0.77 us (2%)
    ppermute x9, starting transfers between devices, across(): return lax.ppermute(values, 'tile', [(t, t ^ hop) for t in range(owners)])  7.35 us
    ppermute x3, waiting for transfers between devices, per_device(): lax.ppermute(values, 'tile', [(t, t ^ 2 * hops[t % 2]) for t in range(own...  6 us
    ppermute x9, waiting for transfers between devices, across(): return lax.ppermute(values, 'tile', [(t, t ^ hop) for t in range(owners)])  5 us
    ppermute x3, starting transfers between devices, per_device(): lax.ppermute(grads, 'grp', [(g, (g + hop) % groups) for g in range(groups)])  4.86 us
    ppermute x3, waiting for transfers between devices, along(): return lax.ppermute(values, 'grp', [(g, g ^ hop) for g in range(groups)])  4.52 us
    ppermute x3, starting transfers between devices, along(): return lax.ppermute(values, 'grp', [(g, g ^ hop) for g in range(groups)])  4.45 us
    ppermute x3, starting transfers between devices, per_device(): lax.ppermute(values, 'tile', [(t, t ^ 2 * hops[t % 2]) for t in range(own...  3.55 us
    unnamed x18, local copies, waits for them, and re-layouts  3.14 us
  transfers between devices with their start and end apart: 18, of which 12 were waited for; matrix products, arithmetic and copies ran while one was open for 0% of the time, Pallas kernels for 3%

commit v1 on v0

--- a/solution.py
+++ b/solution.py
@@ -346,7 +346,7 @@
 
 
 def far_first(groups):
-    return list(range(groups - 1, 0, -1))
+    return list(range(groups // 2, groups)) + list(range(1, groups // 2))
 
 
 def grads_kernel(scale, groups, *refs):

time: 47.2 us -> 47.3 us (level)
  waiting for transfers between devices: 17.9 us -> 18.5 us
  starting transfers between devices: 20.2 us -> 19.7 us
  transfers between devices with their start and end apart: 18 -> 18, of which waited for: 12 -> 13; matrix products, arithmetic and copies ran while one was open for 0% -> 0% of each run, Pallas kernels for 3% -> 3%
where the time goes in v1:
time: 47.3 us; the launch traced here: 47.1 us
  starting transfers between devices  19.7 us (42%)
  waiting for transfers between devices  18.5 us (39%)
  Pallas kernels  4.17 us (9%)
  local copies, waits for them, and re-layouts  3.93 us (8%)
  between operations  0.78 us (2%)
    ppermute x9, starting transfers between devices, across(): return lax.ppermute(values, 'tile', [(t, t ^ hop) for t in range(owners)])  7.36 us
    ppermute x3, waiting for transfers between devices, per_device(): lax.ppermute(values, 'tile', [(t, t ^ 2 * hops[t % 2]) for t in range(own...  6.01 us
    ppermute x9, waiting for transfers between devices, across(): return lax.ppermute(values, 'tile', [(t, t ^ hop) for t in range(owners)])  5 us
    ppermute x3, waiting for transfers between devices, along(): return lax.ppermute(values, 'grp', [(g, g ^ hop) for g in range(groups)])  4.73 us
    ppermute x3, starting transfers between devices, per_device(): lax.ppermute(grads, 'grp', [(g, (g + hop) % groups) for g in range(groups)])  4.58 us
    ppermute x3, starting transfers between devices, along(): return lax.ppermute(values, 'grp', [(g, g ^ hop) for g in range(groups)])  4.23 us
    ppermute x3, starting transfers between devices, per_device(): lax.ppermute(values, 'tile', [(t, t ^ 2 * hops[t % 2]) for t in range(own...  3.55 us
    unnamed x18, local copies, waits for them, and re-layouts  3.14 us
  transfers between devices with their start and end apart: 18, of which 13 were waited for; matrix products, arithmetic and copies ran while one was open for 0% of the time, Pallas kernels for 3%

profile of v1, /device:TPU:0, one launch (start us, length us, event | category | flops | bytes accessed | tf_op | source)
XLA Modules:
  0.0 47.1 jit_solution(12725177759922547665)
XLA Ops:
  0.6 3.0 %collective-permute-start = (f32[4,2,32,128]{3,2,1,0:T(8,128)}, f32[4,2,32,128]{3,2,1,0:T(8,128)S(1)}, u32[]{:S(2)}, u32[]{:S(2)}) collective-permute-start(f32[4,2,32,128]{3,2,1,0:T(8,128)} %speed.1), channel_id=1, source_target_pairs={{0,4},{1,5},{2,6},{3,7},{4,0},{5,1},{6,2},{7,3},{8,12},{9,13},{10,... | collective-permute-start | bytes 393224 | tf_op jit(solution)/shard_map/ppermute | solution.py:381
  3.7 0.1 collective-permute-start.1
  3.7 0.0 collective-permute-start.2
  3.7 1.9 %collective-permute-start.3 = (s32[1,4]{1,0:T(1,128)}, s32[1,4]{1,0:T(1,128)S(1)}, u32[]{:S(2)}, u32[]{:S(2)}) collective-permute-start(s32[1,4]{1,0:T(1,128)} %aperture.1), channel_id=1, source_target_pairs={{0,2},{1,3},{2,0},{3,1},{4,6},{5,7},{6,4},{7,5},{8,10},{9,11},{10,... | collective-permute-start | bytes 56 | tf_op jit(solution)/shard_map/ppermute | solution.py:381
  5.7 0.2 collective-permute-start.4
  5.8 0.0 copy-start.2
  5.8 0.9 %copy-done.2 = f32[4,2,32,128]{3,2,1,0:T(8,128)S(1)} copy-done((f32[4,2,32,128]{3,2,1,0:T(8,128)S(1)}, f32[4,2,32,128]{3,2,1,0:T(8,128)}, u32[]{:S(2)}) %copy-start.2) | copy-done | bytes 131096
  6.7 0.0 copy-start.3
  6.7 0.9 %copy-done.3 = f32[4,2,32,128]{3,2,1,0:T(8,128)S(1)} copy-done((f32[4,2,32,128]{3,2,1,0:T(8,128)S(1)}, f32[4,2,32,128]{3,2,1,0:T(8,128)}, u32[]{:S(2)}) %copy-start.3) | copy-done | bytes 131096
  7.6 0.0 copy-start.6
  7.6 0.7 %copy-done.6 = s32[1,4]{1,0:T(1,128)S(1)} copy-done((s32[1,4]{1,0:T(1,128)S(1)}, s32[1,4]{1,0:T(1,128)}, u32[]{:S(2)}) %copy-start.6) | copy-done | bytes 40
  8.3 0.1 hold_near_tiles.1
  8.4 0.0 collective-permute-done.2.refs_1_
  8.4 0.0 collective-permute-done.3.refs_2_
  8.4 0.4 collective-permute-done.4.refs_3_
  8.8 0.0 collective-permute-done.far_speed
  8.8 1.4 %collective-permute-done.1.far_density = f32[4,2,32,128]{3,2,1,0:T(8,128)S(1)} collective-permute-done((f32[4,2,32,128]{3,2,1,0:T(8,128)}, f32[4,2,32,128]{3,2,1,0:T(8,128)S(1)}, u32[]{:S(2)}, u32[]{:S(2)}) %collective-permute-start.1) | collective-permute-done | bytes 131104 | tf_op jit(solution)/shard_map/ppermute | solution.py:381
  10.2 0.0 copy-start
  10.2 0.0 copy-start.1
  10.2 0.0 copy-start.8
  10.2 0.2 pick_tiles.1
  10.4 0.1 collective-permute-start.5
  10.5 1.8 %collective-permute-start.6 = (f32[2,2,32,128]{3,2,1,0:T(8,128)S(1)}, f32[2,2,32,128]{3,2,1,0:T(8,128)S(1)}, u32[]{:S(2)}, u32[]{:S(2)}) collective-permute-start(f32[2,2,32,128]{3,2,1,0:T(8,128)S(1)} %get-tuple-element.38), channel_id=1, source_target_pairs={{0,2},{1,3},{2,0},{3,1},{4,6},{5,7},{6,4},{7,5},{8,10},{9,11},{10,... | collective-permute-start | bytes 196616 | tf_op jit(solution)/shard_map/ppermute | solution.py:381
  12.3 0.0 copy-start.4
  12.3 0.1 collective-permute-start.7
  12.3 0.0 copy-start.5
  12.3 0.0 copy-start.7
  12.3 0.0 copy-done
  12.4 0.0 copy-done.1
  12.4 0.0 copy-done.8
  12.4 0.6 %copy-done.4 = f32[1,4,8]{2,1,0:T(4,128)S(1)} copy-done((f32[1,4,8]{2,1,0:T(4,128)S(1)}, f32[1,4,8]{2,1,0:T(4,128)}, u32[]{:S(2)}) %copy-start.4) | copy-done | bytes 152
  12.9 0.1 copy-done.5
  13.0 0.0 copy-done.7
  13.0 1.3 %prepare.1 = (f32[3,8,32,128]{3,2,1,0:T(8,128)S(1)}, f32[3,8,32,128]{3,2,1,0:T(8,128)S(1)}, f32[4,8,32,128]{3,2,1,0:T(8,128)S(1)}, f32[4,8,32,128]{3,2,1,0:T(8,1...) custom-call(bf16[1,4,8,32,128]{4,3,2,1,0:T(8,128)(2,1)S(1)} %copy-do, ...), custom_call_target="tpu_custom_call" | custom-call | flops 4000000 | bytes 6000000 | tf_op jit(solution)/shard_map/prepare/pallas_call | solution.py:415
  14.3 0.0 collective-permute-done.5.refs_1_
  14.3 0.7 %collective-permute-done.6.refs_2_ = f32[2,2,32,128]{3,2,1,0:T(8,128)S(1)} collective-permute-done((f32[2,2,32,128]{3,2,1,0:T(8,128)S(1)}, f32[2,2,32,128]{3,2,1,0:T(8,128)S(1)}, u32[]{:S(2)}, u32[]{:S(2)}) %collective-permute-start.6) | collective-permute-done | bytes 65568 | tf_op jit(solution)/shard_map/ppermute | solution.py:381
  15.0 1.3 %collective-permute-done.7.refs_3_ = f32[2,2,32,128]{3,2,1,0:T(8,128)S(1)} collective-permute-done((f32[2,2,32,128]{3,2,1,0:T(8,128)S(1)}, f32[2,2,32,128]{3,2,1,0:T(8,128)S(1)}, u32[]{:S(2)}, u32[]{:S(2)}) %collective-permute-start.7) | collective-permute-done | bytes 65568 | tf_op jit(solution)/shard_map/ppermute | solution.py:381
  16.3 2.4 %replay_and_adjoint.1 = (f32[2,136,128]{2,1,0:T(8,128)S(1)}, f32[2,136,128]{2,1,0:T(8,128)S(1)}, f32[16,48,128]{2,1,0:T(8,128)S(1)}, f32[16,32,128]{2,1,0:T(8,12...) custom-call(f32[2,2,32,128]{3,2,1,0:T(8,128)S(1)} %get-tuple-element, ...), custom_call_target="tpu_custom_call", output_to_operand_aliasing={{2}: (11, {}), {3}: (12, {}), {4}: (13, {}), {5}: (14, {}),... | custom-call | tf_op jit(solution)/shard_map/replay_and_adjoint/pallas_call | solution.py:432
  18.7 0.2 collective-permute-start.8
  18.9 1.2 %collective-permute-done.8.came = f32[2,136,128]{2,1,0:T(8,128)S(1)} collective-permute-done((f32[2,136,128]{2,1,0:T(8,128)S(1)}, f32[2,136,128]{2,1,0:T(8,128)S(1)}, u32[]{:S(2)}, u32[]{:S(2)}) %collective-permute-start.8) | collective-permute-done | bytes 139296 | tf_op jit(solution)/shard_map/ppermute | solution.py:381
  20.1 1.6 %collective-permute-start.10 = (f32[264,128]{1,0:T(8,128)S(1)}, f32[264,128]{1,0:T(8,128)S(1)}, u32[]{:S(2)}, u32[]{:S(2)}) collective-permute-start(f32[264,128]{1,0:T(8,128)S(1)} %get-tuple-element.58), channel_id=1, source_target_pairs={{0,4},{1,7},{2,6},{3,5},{4,0},{5,3},{6,2},{7,1},{8,12},{9,15},{10,... | collective-permute-start | bytes 405512 | tf_op jit(solution)/shard_map/ppermute | solution.py:461
  21.7 1.3 %collective-permute-start.11 = (f32[264,128]{1,0:T(8,128)S(1)}, f32[264,128]{1,0:T(8,128)S(1)}, u32[]{:S(2)}, u32[]{:S(2)}) collective-permute-start(f32[264,128]{1,0:T(8,128)S(1)} %get-tuple-element.59), channel_id=1, source_target_pairs={{0,2},{1,3},{2,0},{3,1},{4,6},{5,7},{6,4},{7,5},{8,10},{9,11},{10,... | collective-permute-start | bytes 405512 | tf_op jit(solution)/shard_map/ppermute | solution.py:461
  23.1 0.6 %collective-permute-start.9 = (f32[264,128]{1,0:T(8,128)S(1)}, f32[264,128]{1,0:T(8,128)S(1)}, u32[]{:S(2)}, u32[]{:S(2)}) collective-permute-start(f32[264,128]{1,0:T(8,128)S(1)} %get-tuple-element.57), channel_id=1, source_target_pairs={{0,6},{1,5},{2,4},{3,7},{4,2},{5,1},{6,0},{7,3},{8,14},{9,13},{10,... | collective-permute-start | bytes 405512 | tf_op jit(solution)/shard_map/ppermute | solution.py:461
  23.7 4.2 %collective-permute-done.10.refs_2_ = f32[264,128]{1,0:T(8,128)S(1)} collective-permute-done((f32[264,128]{1,0:T(8,128)S(1)}, f32[264,128]{1,0:T(8,128)S(1)}, u32[]{:S(2)}, u32[]{:S(2)}) %collective-permute-start.10) | collective-permute-done | bytes 135200 | tf_op jit(solution)/shard_map/ppermute | solution.py:461
  27.9 0.3 collective-permute-done.11.refs_3_
  28.2 1.5 %collective-permute-done.9.refs_1_ = f32[264,128]{1,0:T(8,128)S(1)} collective-permute-done((f32[264,128]{1,0:T(8,128)S(1)}, f32[264,128]{1,0:T(8,128)S(1)}, u32[]{:S(2)}, u32[]{:S(2)}) %collective-permute-start.9) | collective-permute-done | bytes 135200 | tf_op jit(solution)/shard_map/ppermute | solution.py:461
  29.7 0.2 add_stripes.1
  29.9 2.6 %collective-permute-start.12 = (f32[2,64,128]{2,1,0:T(8,128)S(1)}, f32[2,64,128]{2,1,0:T(8,128)S(1)}, u32[]{:S(2)}, u32[]{:S(2)}) collective-permute-start(f32[2,64,128]{2,1,0:T(8,128)S(1)} %get-tuple-element.61), channel_id=1, source_target_pairs={{0,16},{8,24},{16,0},{24,8},{1,17},{9,25},{17,1},{25,9},{2,18},{10... | collective-permute-start | bytes 196616 | tf_op jit(solution)/shard_map/ppermute | solution.py:480
  32.6 1.3 %collective-permute-start.13 = (f32[2,64,128]{2,1,0:T(8,128)S(1)}, f32[2,64,128]{2,1,0:T(8,128)S(1)}, u32[]{:S(2)}, u32[]{:S(2)}) collective-permute-start(f32[2,64,128]{2,1,0:T(8,128)S(1)} %get-tuple-element.62), channel_id=1, source_target_pairs={{0,24},{8,16},{16,8},{24,0},{1,25},{9,17},{17,9},{25,1},{2,26},{10... | collective-permute-start | bytes 196616 | tf_op jit(solution)/shard_map/ppermute | solution.py:480
  33.9 0.2 collective-permute-start.14
  34.1 2.9 %collective-permute-done.12.refs_1_ = f32[2,64,128]{2,1,0:T(8,128)S(1)} collective-permute-done((f32[2,64,128]{2,1,0:T(8,128)S(1)}, f32[2,64,128]{2,1,0:T(8,128)S(1)}, u32[]{:S(2)}, u32[]{:S(2)}) %collective-permute-start.12) | collective-permute-done | bytes 65568 | tf_op jit(solution)/shard_map/ppermute | solution.py:480
  37.0 1.7 %collective-permute-done.13.refs_2_ = f32[2,64,128]{2,1,0:T(8,128)S(1)} collective-permute-done((f32[2,64,128]{2,1,0:T(8,128)S(1)}, f32[2,64,128]{2,1,0:T(8,128)S(1)}, u32[]{:S(2)}, u32[]{:S(2)}) %collective-permute-start.13) | collective-permute-done | bytes 65568 | tf_op jit(solution)/shard_map/ppermute | solution.py:480
  38.7 0.1 collective-permute-done.14.refs_3_
  38.9 0.1 collective-permute-start.15
  39.0 2.8 %collective-permute-start.16 = (f32[2,64,128]{2,1,0:T(8,128)S(1)}, f32[2,64,128]{2,1,0:T(8,128)S(1)}, u32[]{:S(2)}, u32[]{:S(2)}) collective-permute-start(f32[2,64,128]{2,1,0:T(8,128)S(1)} %gradients.1), channel_id=1, source_target_pairs={{0,16},{8,24},{16,0},{24,8},{1,17},{9,25},{17,1},{25,9},{2,18},{10... | collective-permute-start | bytes 196616 | tf_op jit(solution)/shard_map/ppermute | solution.py:496
  41.8 1.7 %collective-permute-start.17 = (f32[2,64,128]{2,1,0:T(8,128)S(1)}, f32[2,64,128]{2,1,0:T(8,128)S(1)}, u32[]{:S(2)}, u32[]{:S(2)}) collective-permute-start(f32[2,64,128]{2,1,0:T(8,128)S(1)} %gradients.1), channel_id=1, source_target_pairs={{0,24},{8,0},{16,8},{24,16},{1,25},{9,1},{17,9},{25,17},{2,26},{10... | collective-permute-start | bytes 196616 | tf_op jit(solution)/shard_map/ppermute | solution.py:496
  43.5 1.7 %collective-permute-done.15 = f32[2,64,128]{2,1,0:T(8,128)S(1)} collective-permute-done((f32[2,64,128]{2,1,0:T(8,128)S(1)}, f32[2,64,128]{2,1,0:T(8,128)S(1)}, u32[]{:S(2)}, u32[]{:S(2)}) %collective-permute-start.15) | collective-permute-done | bytes 65568 | tf_op jit(solution)/shard_map/ppermute | solution.py:496
  45.2 1.1 %collective-permute-done.16 = f32[2,64,128]{2,1,0:T(8,128)S(1)} collective-permute-done((f32[2,64,128]{2,1,0:T(8,128)S(1)}, f32[2,64,128]{2,1,0:T(8,128)S(1)}, u32[]{:S(2)}, u32[]{:S(2)}) %collective-permute-start.16) | collective-permute-done | bytes 65568 | tf_op jit(solution)/shard_map/ppermute | solution.py:496
  46.4 0.0 collective-permute-done.17
  46.4 0.7 %fusion = (f32[1,4,64,128]{3,2,1,0:T(8,128)}, f32[1,4,64,128]{3,2,1,0:T(8,128)}) fusion(f32[2,4,64,128]{3,2,1,0:T(8,128)S(1)} %bitcast_dynamic-update-slice_fusion), kind=kLoop, calls=%fused_computation.4 | loop fusion | bytes 524288 | tf_op jit(solution)/shard_map/slice | solution.py:499
  (8 shorter events, 0.1 us)
Async XLA Ops:
  0.6 8.1 %collective-permute-start = (f32[4,2,32,128]{3,2,1,0:T(8,128)}, f32[4,2,32,128]{3,2,1,0:T(8,128)S(1)}, u32[]{:S(2)}, u32[]{:S(2)}) collective-permute-start(f32[4,2,32,128]{3,2,1,0:T(8,128)} %speed.1), channel_id=1, source_target_pairs={{0,4},{1,5},{2,6},{3,7},{4,0},{5,1},{6,2},{7,3},{8,12},{9,13},{10,... | collective-permute-start | bytes 393224 | tf_op jit(solution)/shard_map/ppermute | solution.py:381
  3.7 6.5 %collective-permute-start.1 = (f32[4,2,32,128]{3,2,1,0:T(8,128)}, f32[4,2,32,128]{3,2,1,0:T(8,128)S(1)}, u32[]{:S(2)}, u32[]{:S(2)}) collective-permute-start(f32[4,2,32,128]{3,2,1,0:T(8,128)} %density.1), channel_id=1, source_target_pairs={{0,4},{1,5},{2,6},{3,7},{4,0},{5,1},{6,2},{7,3},{8,12},{9,13},{10,... | collective-permute-start | bytes 393224 | tf_op jit(solution)/shard_map/ppermute | solution.py:381
  3.7 4.6 %collective-permute-start.2 = (s32[1,4]{1,0:T(1,128)}, s32[1,4]{1,0:T(1,128)S(1)}, u32[]{:S(2)}, u32[]{:S(2)}) collective-permute-start(s32[1,4]{1,0:T(1,128)} %aperture.1), channel_id=1, source_target_pairs={{0,1},{1,0},{2,3},{3,2},{4,5},{5,4},{6,7},{7,6},{8,9},{9,8},{10,11... | collective-permute-start | bytes 56 | tf_op jit(solution)/shard_map/ppermute | solution.py:381
  3.7 4.6 %collective-permute-start.3 = (s32[1,4]{1,0:T(1,128)}, s32[1,4]{1,0:T(1,128)S(1)}, u32[]{:S(2)}, u32[]{:S(2)}) collective-permute-start(s32[1,4]{1,0:T(1,128)} %aperture.1), channel_id=1, source_target_pairs={{0,2},{1,3},{2,0},{3,1},{4,6},{5,7},{6,4},{7,5},{8,10},{9,11},{10,... | collective-permute-start | bytes 56 | tf_op jit(solution)/shard_map/ppermute | solution.py:381
  5.7 3.1 %collective-permute-start.4 = (s32[1,4]{1,0:T(1,128)}, s32[1,4]{1,0:T(1,128)S(1)}, u32[]{:S(2)}, u32[]{:S(2)}) collective-permute-start(s32[1,4]{1,0:T(1,128)} %aperture.1), channel_id=1, source_target_pairs={{0,3},{1,2},{2,1},{3,0},{4,7},{5,6},{6,5},{7,4},{8,11},{9,10},{10,... | collective-permute-start | bytes 56 | tf_op jit(solution)/shard_map/ppermute | solution.py:381
  5.8 0.9 %copy-start.2 = (f32[4,2,32,128]{3,2,1,0:T(8,128)S(1)}, f32[4,2,32,128]{3,2,1,0:T(8,128)}, u32[]{:S(2)}) copy-start(f32[4,2,32,128]{3,2,1,0:T(8,128)} %speed.1) | copy-start | bytes 393220
  6.7 0.9 %copy-start.3 = (f32[4,2,32,128]{3,2,1,0:T(8,128)S(1)}, f32[4,2,32,128]{3,2,1,0:T(8,128)}, u32[]{:S(2)}) copy-start(f32[4,2,32,128]{3,2,1,0:T(8,128)} %density.1) | copy-start | bytes 393220
  7.6 0.7 %copy-start.6 = (s32[1,4]{1,0:T(1,128)S(1)}, s32[1,4]{1,0:T(1,128)}, u32[]{:S(2)}) copy-start(s32[1,4]{1,0:T(1,128)} %aperture.1) | copy-start | bytes 52
  10.2 2.2 %copy-start = (bf16[1,4,8,32,128]{4,3,2,1,0:T(8,128)(2,1)S(1)}, bf16[1,4,8,32,128]{4,3,2,1,0:T(8,128)(2,1)}, u32[]{:S(2)}) copy-start(bf16[1,4,8,32,128]{4,3,2,1,0:T(8,128)(2,1)} %fwd.1) | copy-start | bytes 786436
  10.2 2.2 %copy-start.1 = (bf16[1,4,8,32,128]{4,3,2,1,0:T(8,128)(2,1)S(1)}, bf16[1,4,8,32,128]{4,3,2,1,0:T(8,128)(2,1)}, u32[]{:S(2)}) copy-start(bf16[1,4,8,32,128]{4,3,2,1,0:T(8,128)(2,1)} %adj.1) | copy-start | bytes 786436
  10.2 2.2 %copy-start.8 = (f32[1,4]{1,0:T(1,128)S(1)}, f32[1,4]{1,0:T(1,128)}, u32[]{:S(2)}) copy-start(f32[1,4]{1,0:T(1,128)} %wave.1) | copy-start | bytes 52
  10.4 3.9 %collective-permute-start.5 = (f32[2,2,32,128]{3,2,1,0:T(8,128)S(1)}, f32[2,2,32,128]{3,2,1,0:T(8,128)S(1)}, u32[]{:S(2)}, u32[]{:S(2)}) collective-permute-start(f32[2,2,32,128]{3,2,1,0:T(8,128)S(1)} %get-tuple-element.37), channel_id=1, source_target_pairs={{0,1},{1,0},{2,3},{3,2},{4,5},{5,4},{6,7},{7,6},{8,9},{9,8},{10,11... | collective-permute-start | bytes 196616 | tf_op jit(solution)/shard_map/ppermute | solution.py:381
  10.5 4.5 %collective-permute-start.6 = (f32[2,2,32,128]{3,2,1,0:T(8,128)S(1)}, f32[2,2,32,128]{3,2,1,0:T(8,128)S(1)}, u32[]{:S(2)}, u32[]{:S(2)}) collective-permute-start(f32[2,2,32,128]{3,2,1,0:T(8,128)S(1)} %get-tuple-element.38), channel_id=1, source_target_pairs={{0,2},{1,3},{2,0},{3,1},{4,6},{5,7},{6,4},{7,5},{8,10},{9,11},{10,... | collective-permute-start | bytes 196616 | tf_op jit(solution)/shard_map/ppermute | solution.py:381
  12.3 0.7 %copy-start.4 = (f32[1,4,8]{2,1,0:T(4,128)S(1)}, f32[1,4,8]{2,1,0:T(4,128)}, u32[]{:S(2)}) copy-start(f32[1,4,8]{2,1,0:T(4,128)} %res.1) | copy-start | bytes 388
  12.3 4.0 %collective-permute-start.7 = (f32[2,2,32,128]{3,2,1,0:T(8,128)S(1)}, f32[2,2,32,128]{3,2,1,0:T(8,128)S(1)}, u32[]{:S(2)}, u32[]{:S(2)}) collective-permute-start(f32[2,2,32,128]{3,2,1,0:T(8,128)S(1)} %get-tuple-element.39), channel_id=1, source_target_pairs={{0,3},{1,2},{2,1},{3,0},{4,7},{5,6},{6,5},{7,4},{8,11},{9,10},{10,... | collective-permute-start | bytes 196616 | tf_op jit(solution)/shard_map/ppermute | solution.py:381
  12.3 0.7 %copy-start.5 = (s32[1,8,2]{1,2,0:T(2,128)S(1)}, s32[1,8,2]{1,2,0:T(2,128)}, u32[]{:S(2)}) copy-start(s32[1,8,2]{1,2,0:T(2,128)} %param.16) | copy-start | bytes 196
  12.3 0.7 %copy-start.7 = (s32[1,3]{1,0:T(1,128)S(1)}, s32[1,3]{1,0:T(1,128)}, u32[]{:S(2)}) copy-start(s32[1,3]{1,0:T(1,128)} %src.1) | copy-start | bytes 40
  18.7 1.4 %collective-permute-start.8 = (f32[2,136,128]{2,1,0:T(8,128)S(1)}, f32[2,136,128]{2,1,0:T(8,128)S(1)}, u32[]{:S(2)}, u32[]{:S(2)}) collective-permute-start(f32[2,136,128]{2,1,0:T(8,128)S(1)} %get-tuple-element.55), channel_id=1, source_target_pairs={{0,1},{1,0},{2,3},{3,2},{4,5},{5,4},{6,7},{7,6},{8,9},{9,8},{10,11... | collective-permute-start | bytes 417800 | tf_op jit(solution)/shard_map/ppermute | solution.py:381
  20.1 7.8 %collective-permute-start.10 = (f32[264,128]{1,0:T(8,128)S(1)}, f32[264,128]{1,0:T(8,128)S(1)}, u32[]{:S(2)}, u32[]{:S(2)}) collective-permute-start(f32[264,128]{1,0:T(8,128)S(1)} %get-tuple-element.58), channel_id=1, source_target_pairs={{0,4},{1,7},{2,6},{3,5},{4,0},{5,3},{6,2},{7,1},{8,12},{9,15},{10,... | collective-permute-start | bytes 405512 | tf_op jit(solution)/shard_map/ppermute | solution.py:461
  21.7 6.5 %collective-permute-start.11 = (f32[264,128]{1,0:T(8,128)S(1)}, f32[264,128]{1,0:T(8,128)S(1)}, u32[]{:S(2)}, u32[]{:S(2)}) collective-permute-start(f32[264,128]{1,0:T(8,128)S(1)} %get-tuple-element.59), channel_id=1, source_target_pairs={{0,2},{1,3},{2,0},{3,1},{4,6},{5,7},{6,4},{7,5},{8,10},{9,11},{10,... | collective-permute-start | bytes 405512 | tf_op jit(solution)/shard_map/ppermute | solution.py:461
  23.1 6.6 %collective-permute-start.9 = (f32[264,128]{1,0:T(8,128)S(1)}, f32[264,128]{1,0:T(8,128)S(1)}, u32[]{:S(2)}, u32[]{:S(2)}) collective-permute-start(f32[264,128]{1,0:T(8,128)S(1)} %get-tuple-element.57), channel_id=1, source_target_pairs={{0,6},{1,5},{2,4},{3,7},{4,2},{5,1},{6,0},{7,3},{8,14},{9,13},{10,... | collective-permute-start | bytes 405512 | tf_op jit(solution)/shard_map/ppermute | solution.py:461
  29.9 7.1 %collective-permute-start.12 = (f32[2,64,128]{2,1,0:T(8,128)S(1)}, f32[2,64,128]{2,1,0:T(8,128)S(1)}, u32[]{:S(2)}, u32[]{:S(2)}) collective-permute-start(f32[2,64,128]{2,1,0:T(8,128)S(1)} %get-tuple-element.61), channel_id=1, source_target_pairs={{0,16},{8,24},{16,0},{24,8},{1,17},{9,25},{17,1},{25,9},{2,18},{10... | collective-permute-start | bytes 196616 | tf_op jit(solution)/shard_map/ppermute | solution.py:480
  32.6 6.2 %collective-permute-start.13 = (f32[2,64,128]{2,1,0:T(8,128)S(1)}, f32[2,64,128]{2,1,0:T(8,128)S(1)}, u32[]{:S(2)}, u32[]{:S(2)}) collective-permute-start(f32[2,64,128]{2,1,0:T(8,128)S(1)} %get-tuple-element.62), channel_id=1, source_target_pairs={{0,24},{8,16},{16,8},{24,0},{1,25},{9,17},{17,9},{25,1},{2,26},{10... | collective-permute-start | bytes 196616 | tf_op jit(solution)/shard_map/ppermute | solution.py:480
  33.9 5.0 %collective-permute-start.14 = (f32[2,64,128]{2,1,0:T(8,128)S(1)}, f32[2,64,128]{2,1,0:T(8,128)S(1)}, u32[]{:S(2)}, u32[]{:S(2)}) collective-permute-start(f32[2,64,128]{2,1,0:T(8,128)S(1)} %get-tuple-element.63), channel_id=1, source_target_pairs={{0,8},{8,0},{16,24},{24,16},{1,9},{9,1},{17,25},{25,17},{2,10},{10... | collective-permute-start | bytes 196616 | tf_op jit(solution)/shard_map/ppermute | solution.py:480
  38.9 6.3 %collective-permute-start.15 = (f32[2,64,128]{2,1,0:T(8,128)S(1)}, f32[2,64,128]{2,1,0:T(8,128)S(1)}, u32[]{:S(2)}, u32[]{:S(2)}) collective-permute-start(f32[2,64,128]{2,1,0:T(8,128)S(1)} %gradients.1), channel_id=1, source_target_pairs={{0,8},{8,16},{16,24},{24,0},{1,9},{9,17},{17,25},{25,1},{2,10},{10... | collective-permute-start | bytes 196616 | tf_op jit(solution)/shard_map/ppermute | solution.py:496
  39.0 7.4 %collective-permute-start.16 = (f32[2,64,128]{2,1,0:T(8,128)S(1)}, f32[2,64,128]{2,1,0:T(8,128)S(1)}, u32[]{:S(2)}, u32[]{:S(2)}) collective-permute-start(f32[2,64,128]{2,1,0:T(8,128)S(1)} %gradients.1), channel_id=1, source_target_pairs={{0,16},{8,24},{16,0},{24,8},{1,17},{9,25},{17,1},{25,9},{2,18},{10... | collective-permute-start | bytes 196616 | tf_op jit(solution)/shard_map/ppermute | solution.py:496
  41.8 4.6 %collective-permute-start.17 = (f32[2,64,128]{2,1,0:T(8,128)S(1)}, f32[2,64,128]{2,1,0:T(8,128)S(1)}, u32[]{:S(2)}, u32[]{:S(2)}) collective-permute-start(f32[2,64,128]{2,1,0:T(8,128)S(1)} %gradients.1), channel_id=1, source_target_pairs={{0,24},{8,0},{16,8},{24,16},{1,25},{9,1},{17,9},{25,17},{2,26},{10... | collective-permute-start | bytes 196616 | tf_op jit(solution)/shard_map/ppermute | solution.py:496

commit v2 on v0

--- a/solution.py
+++ b/solution.py
@@ -181,6 +181,10 @@
             piece[1] = far_density[column]
 
 
+def gather_order(stripes):
+    return [0] + list(range(2, stripes, 2)) + list(range(1, stripes, 2))
+
+
 def wave_kernel(chips, steps, held, *refs):
     stripes = 2 * chips
     pieces, refs = refs[:stripes], refs[stripes:]
@@ -196,9 +200,9 @@
     def place_of(hop):
         return lax.rem((residue ^ hop) - corner + stripes, stripes) * tile_x
 
-    for hop in range(stripes):
+    for hop, piece in zip(gather_order(stripes), pieces):
         cells = pl.ds(place_of(hop), tile_x)
-        speed, density = pieces[hop][0], pieces[hop][1]
+        speed, density = piece[0], piece[1]
         bulk[cells] = COEF[0] * (density * speed * speed)
         buoy[cells] = COEF[0] / density
 
@@ -410,7 +414,6 @@
         compiler_params=PARAMS,
         name="pick_tiles",
     )(near_speed, near_density, far_speed, far_density, entry, *[lists[h] for h in range(1, stripes)])
-    moved = {hop: across(pieces[hop], hop) for hop in range(stripes - 1, 0, -1)}
 
     prepared = pl.pallas_call(
         functools.partial(prepare_kernel, steps),
@@ -425,7 +428,7 @@
         name="prepare",
     )(fwd_state, adj_state, src_pos, wavelet, jnp.swapaxes(rec_pos, 1, 2), residual, pieces[0])
     prepared, fields = prepared[:6], prepared[6:]
-    pieces = [pieces[0]] + [moved[hop] for hop in range(1, stripes)]
+    pieces = [across(pieces[hop], hop) if hop else pieces[0] for hop in gather_order(stripes)]
 
     tile_rows = tile_x * tile_y
     sent = shape(chips, 2 * tile_rows + 8, depth)

time: 47.2 us -> 47.3 us (level)
  starting transfers between devices: 20.2 us -> 20.7 us
    ppermute x9, waiting for transfers between devices: 5 us -> 4.16 us  [across(): return lax.ppermute(values, 'tile', [(t, t ^ hop) for t in range(owners)])]
    ppermute x9, starting transfers between devices: 7.35 us -> 7.93 us  [across(): return lax.ppermute(values, 'tile', [(t, t ^ hop) for t in range(owners)])]
where the time goes in v2:
time: 47.3 us; the launch traced here: 47.1 us
  starting transfers between devices  20.7 us (44%)
  waiting for transfers between devices  17.5 us (37%)
  Pallas kernels  4.17 us (9%)
  local copies, waits for them, and re-layouts  3.93 us (8%)
  between operations  0.76 us (2%)
    ppermute x9, starting transfers between devices, across(): return lax.ppermute(values, 'tile', [(t, t ^ hop) for t in range(owners)])  7.93 us
    ppermute x3, waiting for transfers between devices, per_device(): lax.ppermute(values, 'tile', [(t, t ^ 2 * hops[t % 2]) for t in range(own...  6.21 us
    ppermute x3, starting transfers between devices, per_device(): lax.ppermute(grads, 'grp', [(g, (g + hop) % groups) for g in range(groups)])  4.8 us
    ppermute x3, waiting for transfers between devices, along(): return lax.ppermute(values, 'grp', [(g, g ^ hop) for g in range(groups)])  4.57 us
    ppermute x3, starting transfers between devices, along(): return lax.ppermute(values, 'grp', [(g, g ^ hop) for g in range(groups)])  4.45 us
    ppermute x9, waiting for transfers between devices, across(): return lax.ppermute(values, 'tile', [(t, t ^ hop) for t in range(owners)])  4.16 us
    ppermute x3, starting transfers between devices, per_device(): lax.ppermute(values, 'tile', [(t, t ^ 2 * hops[t % 2]) for t in range(own...  3.55 us
    unnamed x18, local copies, waits for them, and re-layouts  3.14 us
  transfers between devices with their start and end apart: 18, of which 12 were waited for; matrix products, arithmetic and copies ran while one was open for 0% of the time, Pallas kernels for 3%

profile of v2, /device:TPU:0, one launch (start us, length us, event | category | flops | bytes accessed | tf_op | source)
XLA Modules:
  0.0 47.1 jit_solution(3151650046420364033)
XLA Ops:
  0.6 3.0 %collective-permute-start = (f32[4,2,32,128]{3,2,1,0:T(8,128)}, f32[4,2,32,128]{3,2,1,0:T(8,128)S(1)}, u32[]{:S(2)}, u32[]{:S(2)}) collective-permute-start(f32[4,2,32,128]{3,2,1,0:T(8,128)} %speed.1), channel_id=1, source_target_pairs={{0,4},{1,5},{2,6},{3,7},{4,0},{5,1},{6,2},{7,3},{8,12},{9,13},{10,... | collective-permute-start | bytes 393224 | tf_op jit(solution)/shard_map/ppermute | solution.py:385
  3.7 0.1 collective-permute-start.1
  3.7 0.0 collective-permute-start.2
  3.7 1.9 %collective-permute-start.3 = (s32[1,4]{1,0:T(1,128)}, s32[1,4]{1,0:T(1,128)S(1)}, u32[]{:S(2)}, u32[]{:S(2)}) collective-permute-start(s32[1,4]{1,0:T(1,128)} %aperture.1), channel_id=1, source_target_pairs={{0,2},{1,3},{2,0},{3,1},{4,6},{5,7},{6,4},{7,5},{8,10},{9,11},{10,... | collective-permute-start | bytes 56 | tf_op jit(solution)/shard_map/ppermute | solution.py:385
  5.7 0.2 collective-permute-start.4
  5.8 0.0 copy-start.2
  5.8 0.9 %copy-done.2 = f32[4,2,32,128]{3,2,1,0:T(8,128)S(1)} copy-done((f32[4,2,32,128]{3,2,1,0:T(8,128)S(1)}, f32[4,2,32,128]{3,2,1,0:T(8,128)}, u32[]{:S(2)}) %copy-start.2) | copy-done | bytes 131096
  6.7 0.0 copy-start.3
  6.7 0.9 %copy-done.3 = f32[4,2,32,128]{3,2,1,0:T(8,128)S(1)} copy-done((f32[4,2,32,128]{3,2,1,0:T(8,128)S(1)}, f32[4,2,32,128]{3,2,1,0:T(8,128)}, u32[]{:S(2)}) %copy-start.3) | copy-done | bytes 131096
  7.6 0.0 copy-start.6
  7.6 0.7 %copy-done.6 = s32[1,4]{1,0:T(1,128)S(1)} copy-done((s32[1,4]{1,0:T(1,128)S(1)}, s32[1,4]{1,0:T(1,128)}, u32[]{:S(2)}) %copy-start.6) | copy-done | bytes 40
  8.3 0.1 hold_near_tiles.1
  8.4 0.0 collective-permute-done.2.refs_1_
  8.4 0.0 collective-permute-done.3.refs_2_
  8.4 0.4 collective-permute-done.4.refs_3_
  8.8 0.0 collective-permute-done.far_speed
  8.8 1.4 %collective-permute-done.1.far_density = f32[4,2,32,128]{3,2,1,0:T(8,128)S(1)} collective-permute-done((f32[4,2,32,128]{3,2,1,0:T(8,128)}, f32[4,2,32,128]{3,2,1,0:T(8,128)S(1)}, u32[]{:S(2)}, u32[]{:S(2)}) %collective-permute-start.1) | collective-permute-done | bytes 131104 | tf_op jit(solution)/shard_map/ppermute | solution.py:385
  10.2 0.0 copy-start
  10.2 0.0 copy-start.1
  10.2 0.0 copy-start.8
  10.2 0.2 pick_tiles.1
  10.4 1.8 %collective-permute-start.5 = (f32[2,2,32,128]{3,2,1,0:T(8,128)S(1)}, f32[2,2,32,128]{3,2,1,0:T(8,128)S(1)}, u32[]{:S(2)}, u32[]{:S(2)}) collective-permute-start(f32[2,2,32,128]{3,2,1,0:T(8,128)S(1)} %get-tuple-element.37), channel_id=1, source_target_pairs={{0,2},{1,3},{2,0},{3,1},{4,6},{5,7},{6,4},{7,5},{8,10},{9,11},{10,... | collective-permute-start | bytes 196616 | tf_op jit(solution)/shard_map/ppermute | solution.py:385
  12.2 0.0 collective-permute-start.6
  12.2 0.0 copy-start.4
  12.2 0.4 collective-permute-start.7
  12.6 0.0 copy-start.5
  12.6 0.0 copy-start.7
  12.6 0.0 copy-done
  12.6 0.0 copy-done.1
  12.6 0.0 copy-done.8
  12.6 0.2 copy-done.4
  12.9 0.4 copy-done.5
  13.3 0.0 copy-done.7
  13.3 1.3 %prepare.1 = (f32[3,8,32,128]{3,2,1,0:T(8,128)S(1)}, f32[3,8,32,128]{3,2,1,0:T(8,128)S(1)}, f32[4,8,32,128]{3,2,1,0:T(8,128)S(1)}, f32[4,8,32,128]{3,2,1,0:T(8,1...) custom-call(bf16[1,4,8,32,128]{4,3,2,1,0:T(8,128)(2,1)S(1)} %copy-do, ...), custom_call_target="tpu_custom_call" | custom-call | flops 4000000 | bytes 6000000 | tf_op jit(solution)/shard_map/prepare/pallas_call | solution.py:418
  14.6 0.2 collective-permute-done.5.refs_1_
  14.7 0.0 collective-permute-done.6.refs_2_
  14.7 1.2 %collective-permute-done.7.refs_3_ = f32[2,2,32,128]{3,2,1,0:T(8,128)S(1)} collective-permute-done((f32[2,2,32,128]{3,2,1,0:T(8,128)S(1)}, f32[2,2,32,128]{3,2,1,0:T(8,128)S(1)}, u32[]{:S(2)}, u32[]{:S(2)}) %collective-permute-start.7) | collective-permute-done | bytes 65568 | tf_op jit(solution)/shard_map/ppermute | solution.py:385
  15.9 2.4 %replay_and_adjoint.1 = (f32[2,136,128]{2,1,0:T(8,128)S(1)}, f32[2,136,128]{2,1,0:T(8,128)S(1)}, f32[16,48,128]{2,1,0:T(8,128)S(1)}, f32[16,32,128]{2,1,0:T(8,12...) custom-call(f32[2,2,32,128]{3,2,1,0:T(8,128)S(1)} %get-tuple-element, ...), custom_call_target="tpu_custom_call", output_to_operand_aliasing={{2}: (11, {}), {3}: (12, {}), {4}: (13, {}), {5}: (14, {}),... | custom-call | tf_op jit(solution)/shard_map/replay_and_adjoint/pallas_call | solution.py:435
  18.3 0.5 %collective-permute-start.8 = (f32[2,136,128]{2,1,0:T(8,128)S(1)}, f32[2,136,128]{2,1,0:T(8,128)S(1)}, u32[]{:S(2)}, u32[]{:S(2)}) collective-permute-start(f32[2,136,128]{2,1,0:T(8,128)S(1)} %get-tuple-element.55), channel_id=1, source_target_pairs={{0,1},{1,0},{2,3},{3,2},{4,5},{5,4},{6,7},{7,6},{8,9},{9,8},{10,11... | collective-permute-start | bytes 417800 | tf_op jit(solution)/shard_map/ppermute | solution.py:385
  18.8 1.0 %collective-permute-done.8.came = f32[2,136,128]{2,1,0:T(8,128)S(1)} collective-permute-done((f32[2,136,128]{2,1,0:T(8,128)S(1)}, f32[2,136,128]{2,1,0:T(8,128)S(1)}, u32[]{:S(2)}, u32[]{:S(2)}) %collective-permute-start.8) | collective-permute-done | bytes 139296 | tf_op jit(solution)/shard_map/ppermute | solution.py:385
  19.9 1.6 %collective-permute-start.10 = (f32[264,128]{1,0:T(8,128)S(1)}, f32[264,128]{1,0:T(8,128)S(1)}, u32[]{:S(2)}, u32[]{:S(2)}) collective-permute-start(f32[264,128]{1,0:T(8,128)S(1)} %get-tuple-element.58), channel_id=1, source_target_pairs={{0,4},{1,7},{2,6},{3,5},{4,0},{5,3},{6,2},{7,1},{8,12},{9,15},{10,... | collective-permute-start | bytes 405512 | tf_op jit(solution)/shard_map/ppermute | solution.py:464
  21.4 1.2 %collective-permute-start.11 = (f32[264,128]{1,0:T(8,128)S(1)}, f32[264,128]{1,0:T(8,128)S(1)}, u32[]{:S(2)}, u32[]{:S(2)}) collective-permute-start(f32[264,128]{1,0:T(8,128)S(1)} %get-tuple-element.59), channel_id=1, source_target_pairs={{0,2},{1,3},{2,0},{3,1},{4,6},{5,7},{6,4},{7,5},{8,10},{9,11},{10,... | collective-permute-start | bytes 405512 | tf_op jit(solution)/shard_map/ppermute | solution.py:464
  22.7 0.7 %collective-permute-start.9 = (f32[264,128]{1,0:T(8,128)S(1)}, f32[264,128]{1,0:T(8,128)S(1)}, u32[]{:S(2)}, u32[]{:S(2)}) collective-permute-start(f32[264,128]{1,0:T(8,128)S(1)} %get-tuple-element.57), channel_id=1, source_target_pairs={{0,6},{1,5},{2,4},{3,7},{4,2},{5,1},{6,0},{7,3},{8,14},{9,13},{10,... | collective-permute-start | bytes 405512 | tf_op jit(solution)/shard_map/ppermute | solution.py:464
  23.4 3.8 %collective-permute-done.10.refs_2_ = f32[264,128]{1,0:T(8,128)S(1)} collective-permute-done((f32[264,128]{1,0:T(8,128)S(1)}, f32[264,128]{1,0:T(8,128)S(1)}, u32[]{:S(2)}, u32[]{:S(2)}) %collective-permute-start.10) | collective-permute-done | bytes 135200 | tf_op jit(solution)/shard_map/ppermute | solution.py:464
  27.3 0.7 %collective-permute-done.11.refs_3_ = f32[264,128]{1,0:T(8,128)S(1)} collective-permute-done((f32[264,128]{1,0:T(8,128)S(1)}, f32[264,128]{1,0:T(8,128)S(1)}, u32[]{:S(2)}, u32[]{:S(2)}) %collective-permute-start.11) | collective-permute-done | bytes 135200 | tf_op jit(solution)/shard_map/ppermute | solution.py:464
  27.9 1.7 %collective-permute-done.9.refs_1_ = f32[264,128]{1,0:T(8,128)S(1)} collective-permute-done((f32[264,128]{1,0:T(8,128)S(1)}, f32[264,128]{1,0:T(8,128)S(1)}, u32[]{:S(2)}, u32[]{:S(2)}) %collective-permute-start.9) | collective-permute-done | bytes 135200 | tf_op jit(solution)/shard_map/ppermute | solution.py:464
  29.6 0.2 add_stripes.1
  29.8 3.7 %collective-permute-start.12 = (f32[2,64,128]{2,1,0:T(8,128)S(1)}, f32[2,64,128]{2,1,0:T(8,128)S(1)}, u32[]{:S(2)}, u32[]{:S(2)}) collective-permute-start(f32[2,64,128]{2,1,0:T(8,128)S(1)} %get-tuple-element.61), channel_id=1, source_target_pairs={{0,24},{8,16},{16,8},{24,0},{1,25},{9,17},{17,9},{25,1},{2,26},{10... | collective-permute-start | bytes 196616 | tf_op jit(solution)/shard_map/ppermute | solution.py:483
  33.5 0.0 collective-permute-start.13
  33.5 0.8 %collective-permute-start.14 = (f32[2,64,128]{2,1,0:T(8,128)S(1)}, f32[2,64,128]{2,1,0:T(8,128)S(1)}, u32[]{:S(2)}, u32[]{:S(2)}) collective-permute-start(f32[2,64,128]{2,1,0:T(8,128)S(1)} %get-tuple-element.63), channel_id=1, source_target_pairs={{0,8},{8,0},{16,24},{24,16},{1,9},{9,1},{17,25},{25,17},{2,10},{10... | collective-permute-start | bytes 196616 | tf_op jit(solution)/shard_map/ppermute | solution.py:483
  34.3 2.0 %collective-permute-done.12.refs_1_ = f32[2,64,128]{2,1,0:T(8,128)S(1)} collective-permute-done((f32[2,64,128]{2,1,0:T(8,128)S(1)}, f32[2,64,128]{2,1,0:T(8,128)S(1)}, u32[]{:S(2)}, u32[]{:S(2)}) %collective-permute-start.12) | collective-permute-done | bytes 65568 | tf_op jit(solution)/shard_map/ppermute | solution.py:483
  36.3 2.6 %collective-permute-done.13.refs_2_ = f32[2,64,128]{2,1,0:T(8,128)S(1)} collective-permute-done((f32[2,64,128]{2,1,0:T(8,128)S(1)}, f32[2,64,128]{2,1,0:T(8,128)S(1)}, u32[]{:S(2)}, u32[]{:S(2)}) %collective-permute-start.13) | collective-permute-done | bytes 65568 | tf_op jit(solution)/shard_map/ppermute | solution.py:483
  38.9 0.0 collective-permute-done.14.refs_3_
  38.9 0.6 %collective-permute-start.15 = (f32[2,64,128]{2,1,0:T(8,128)S(1)}, f32[2,64,128]{2,1,0:T(8,128)S(1)}, u32[]{:S(2)}, u32[]{:S(2)}) collective-permute-start(f32[2,64,128]{2,1,0:T(8,128)S(1)} %gradients.1), channel_id=1, source_target_pairs={{0,8},{8,16},{16,24},{24,0},{1,9},{9,17},{17,25},{25,1},{2,10},{10... | collective-permute-start | bytes 196616 | tf_op jit(solution)/shard_map/ppermute | solution.py:499
  39.5 2.3 %collective-permute-start.16 = (f32[2,64,128]{2,1,0:T(8,128)S(1)}, f32[2,64,128]{2,1,0:T(8,128)S(1)}, u32[]{:S(2)}, u32[]{:S(2)}) collective-permute-start(f32[2,64,128]{2,1,0:T(8,128)S(1)} %gradients.1), channel_id=1, source_target_pairs={{0,16},{8,24},{16,0},{24,8},{1,17},{9,25},{17,1},{25,9},{2,18},{10... | collective-permute-start | bytes 196616 | tf_op jit(solution)/shard_map/ppermute | solution.py:499
  41.8 1.9 %collective-permute-start.17 = (f32[2,64,128]{2,1,0:T(8,128)S(1)}, f32[2,64,128]{2,1,0:T(8,128)S(1)}, u32[]{:S(2)}, u32[]{:S(2)}) collective-permute-start(f32[2,64,128]{2,1,0:T(8,128)S(1)} %gradients.1), channel_id=1, source_target_pairs={{0,24},{8,0},{16,8},{24,16},{1,25},{9,1},{17,9},{25,17},{2,26},{10... | collective-permute-start | bytes 196616 | tf_op jit(solution)/shard_map/ppermute | solution.py:499
  43.7 1.4 %collective-permute-done.15 = f32[2,64,128]{2,1,0:T(8,128)S(1)} collective-permute-done((f32[2,64,128]{2,1,0:T(8,128)S(1)}, f32[2,64,128]{2,1,0:T(8,128)S(1)}, u32[]{:S(2)}, u32[]{:S(2)}) %collective-permute-start.15) | collective-permute-done | bytes 65568 | tf_op jit(solution)/shard_map/ppermute | solution.py:499
  45.1 1.2 %collective-permute-done.16 = f32[2,64,128]{2,1,0:T(8,128)S(1)} collective-permute-done((f32[2,64,128]{2,1,0:T(8,128)S(1)}, f32[2,64,128]{2,1,0:T(8,128)S(1)}, u32[]{:S(2)}, u32[]{:S(2)}) %collective-permute-start.16) | collective-permute-done | bytes 65568 | tf_op jit(solution)/shard_map/ppermute | solution.py:499
  46.3 0.0 collective-permute-done.17
  46.4 0.7 %fusion = (f32[1,4,64,128]{3,2,1,0:T(8,128)}, f32[1,4,64,128]{3,2,1,0:T(8,128)}) fusion(f32[2,4,64,128]{3,2,1,0:T(8,128)S(1)} %bitcast_dynamic-update-slice_fusion), kind=kLoop, calls=%fused_computation.4 | loop fusion | bytes 524288 | tf_op jit(solution)/shard_map/slice | solution.py:502
  (8 shorter events, 0.1 us)
Async XLA Ops:
  0.6 8.1 %collective-permute-start = (f32[4,2,32,128]{3,2,1,0:T(8,128)}, f32[4,2,32,128]{3,2,1,0:T(8,128)S(1)}, u32[]{:S(2)}, u32[]{:S(2)}) collective-permute-start(f32[4,2,32,128]{3,2,1,0:T(8,128)} %speed.1), channel_id=1, source_target_pairs={{0,4},{1,5},{2,6},{3,7},{4,0},{5,1},{6,2},{7,3},{8,12},{9,13},{10,... | collective-permute-start | bytes 393224 | tf_op jit(solution)/shard_map/ppermute | solution.py:385
  3.7 6.5 %collective-permute-start.1 = (f32[4,2,32,128]{3,2,1,0:T(8,128)}, f32[4,2,32,128]{3,2,1,0:T(8,128)S(1)}, u32[]{:S(2)}, u32[]{:S(2)}) collective-permute-start(f32[4,2,32,128]{3,2,1,0:T(8,128)} %density.1), channel_id=1, source_target_pairs={{0,4},{1,5},{2,6},{3,7},{4,0},{5,1},{6,2},{7,3},{8,12},{9,13},{10,... | collective-permute-start | bytes 393224 | tf_op jit(solution)/shard_map/ppermute | solution.py:385
  3.7 4.6 %collective-permute-start.2 = (s32[1,4]{1,0:T(1,128)}, s32[1,4]{1,0:T(1,128)S(1)}, u32[]{:S(2)}, u32[]{:S(2)}) collective-permute-start(s32[1,4]{1,0:T(1,128)} %aperture.1), channel_id=1, source_target_pairs={{0,1},{1,0},{2,3},{3,2},{4,5},{5,4},{6,7},{7,6},{8,9},{9,8},{10,11... | collective-permute-start | bytes 56 | tf_op jit(solution)/shard_map/ppermute | solution.py:385
  3.7 4.6 %collective-permute-start.3 = (s32[1,4]{1,0:T(1,128)}, s32[1,4]{1,0:T(1,128)S(1)}, u32[]{:S(2)}, u32[]{:S(2)}) collective-permute-start(s32[1,4]{1,0:T(1,128)} %aperture.1), channel_id=1, source_target_pairs={{0,2},{1,3},{2,0},{3,1},{4,6},{5,7},{6,4},{7,5},{8,10},{9,11},{10,... | collective-permute-start | bytes 56 | tf_op jit(solution)/shard_map/ppermute | solution.py:385
  5.7 3.1 %collective-permute-start.4 = (s32[1,4]{1,0:T(1,128)}, s32[1,4]{1,0:T(1,128)S(1)}, u32[]{:S(2)}, u32[]{:S(2)}) collective-permute-start(s32[1,4]{1,0:T(1,128)} %aperture.1), channel_id=1, source_target_pairs={{0,3},{1,2},{2,1},{3,0},{4,7},{5,6},{6,5},{7,4},{8,11},{9,10},{10,... | collective-permute-start | bytes 56 | tf_op jit(solution)/shard_map/ppermute | solution.py:385
  5.8 0.9 %copy-start.2 = (f32[4,2,32,128]{3,2,1,0:T(8,128)S(1)}, f32[4,2,32,128]{3,2,1,0:T(8,128)}, u32[]{:S(2)}) copy-start(f32[4,2,32,128]{3,2,1,0:T(8,128)} %speed.1) | copy-start | bytes 393220
  6.7 0.9 %copy-start.3 = (f32[4,2,32,128]{3,2,1,0:T(8,128)S(1)}, f32[4,2,32,128]{3,2,1,0:T(8,128)}, u32[]{:S(2)}) copy-start(f32[4,2,32,128]{3,2,1,0:T(8,128)} %density.1) | copy-start | bytes 393220
  7.6 0.7 %copy-start.6 = (s32[1,4]{1,0:T(1,128)S(1)}, s32[1,4]{1,0:T(1,128)}, u32[]{:S(2)}) copy-start(s32[1,4]{1,0:T(1,128)} %aperture.1) | copy-start | bytes 52
  10.2 2.4 %copy-start = (bf16[1,4,8,32,128]{4,3,2,1,0:T(8,128)(2,1)S(1)}, bf16[1,4,8,32,128]{4,3,2,1,0:T(8,128)(2,1)}, u32[]{:S(2)}) copy-start(bf16[1,4,8,32,128]{4,3,2,1,0:T(8,128)(2,1)} %fwd.1) | copy-start | bytes 786436
  10.2 2.4 %copy-start.1 = (bf16[1,4,8,32,128]{4,3,2,1,0:T(8,128)(2,1)S(1)}, bf16[1,4,8,32,128]{4,3,2,1,0:T(8,128)(2,1)}, u32[]{:S(2)}) copy-start(bf16[1,4,8,32,128]{4,3,2,1,0:T(8,128)(2,1)} %adj.1) | copy-start | bytes 786436
  10.2 2.4 %copy-start.8 = (f32[1,4]{1,0:T(1,128)S(1)}, f32[1,4]{1,0:T(1,128)}, u32[]{:S(2)}) copy-start(f32[1,4]{1,0:T(1,128)} %wave.1) | copy-start | bytes 52
  10.4 4.3 %collective-permute-start.5 = (f32[2,2,32,128]{3,2,1,0:T(8,128)S(1)}, f32[2,2,32,128]{3,2,1,0:T(8,128)S(1)}, u32[]{:S(2)}, u32[]{:S(2)}) collective-permute-start(f32[2,2,32,128]{3,2,1,0:T(8,128)S(1)} %get-tuple-element.37), channel_id=1, source_target_pairs={{0,2},{1,3},{2,0},{3,1},{4,6},{5,7},{6,4},{7,5},{8,10},{9,11},{10,... | collective-permute-start | bytes 196616 | tf_op jit(solution)/shard_map/ppermute | solution.py:385
  12.2 2.6 %collective-permute-start.6 = (f32[2,2,32,128]{3,2,1,0:T(8,128)S(1)}, f32[2,2,32,128]{3,2,1,0:T(8,128)S(1)}, u32[]{:S(2)}, u32[]{:S(2)}) collective-permute-start(f32[2,2,32,128]{3,2,1,0:T(8,128)S(1)} %get-tuple-element.38), channel_id=1, source_target_pairs={{0,1},{1,0},{2,3},{3,2},{4,5},{5,4},{6,7},{7,6},{8,9},{9,8},{10,11... | collective-permute-start | bytes 196616 | tf_op jit(solution)/shard_map/ppermute | solution.py:385
  12.2 0.7 %copy-start.4 = (f32[1,4,8]{2,1,0:T(4,128)S(1)}, f32[1,4,8]{2,1,0:T(4,128)}, u32[]{:S(2)}) copy-start(f32[1,4,8]{2,1,0:T(4,128)} %res.1) | copy-start | bytes 388
  12.2 3.7 %collective-permute-start.7 = (f32[2,2,32,128]{3,2,1,0:T(8,128)S(1)}, f32[2,2,32,128]{3,2,1,0:T(8,128)S(1)}, u32[]{:S(2)}, u32[]{:S(2)}) collective-permute-start(f32[2,2,32,128]{3,2,1,0:T(8,128)S(1)} %get-tuple-element.39), channel_id=1, source_target_pairs={{0,3},{1,2},{2,1},{3,0},{4,7},{5,6},{6,5},{7,4},{8,11},{9,10},{10,... | collective-permute-start | bytes 196616 | tf_op jit(solution)/shard_map/ppermute | solution.py:385
  12.6 0.7 %copy-start.5 = (s32[1,8,2]{1,2,0:T(2,128)S(1)}, s32[1,8,2]{1,2,0:T(2,128)}, u32[]{:S(2)}) copy-start(s32[1,8,2]{1,2,0:T(2,128)} %param.16) | copy-start | bytes 196
  12.6 0.7 %copy-start.7 = (s32[1,3]{1,0:T(1,128)S(1)}, s32[1,3]{1,0:T(1,128)}, u32[]{:S(2)}) copy-start(s32[1,3]{1,0:T(1,128)} %src.1) | copy-start | bytes 40
  18.3 1.5 %collective-permute-start.8 = (f32[2,136,128]{2,1,0:T(8,128)S(1)}, f32[2,136,128]{2,1,0:T(8,128)S(1)}, u32[]{:S(2)}, u32[]{:S(2)}) collective-permute-start(f32[2,136,128]{2,1,0:T(8,128)S(1)} %get-tuple-element.55), channel_id=1, source_target_pairs={{0,1},{1,0},{2,3},{3,2},{4,5},{5,4},{6,7},{7,6},{8,9},{9,8},{10,11... | collective-permute-start | bytes 417800 | tf_op jit(solution)/shard_map/ppermute | solution.py:385
  19.9 7.4 %collective-permute-start.10 = (f32[264,128]{1,0:T(8,128)S(1)}, f32[264,128]{1,0:T(8,128)S(1)}, u32[]{:S(2)}, u32[]{:S(2)}) collective-permute-start(f32[264,128]{1,0:T(8,128)S(1)} %get-tuple-element.58), channel_id=1, source_target_pairs={{0,4},{1,7},{2,6},{3,5},{4,0},{5,3},{6,2},{7,1},{8,12},{9,15},{10,... | collective-permute-start | bytes 405512 | tf_op jit(solution)/shard_map/ppermute | solution.py:464
  21.4 6.5 %collective-permute-start.11 = (f32[264,128]{1,0:T(8,128)S(1)}, f32[264,128]{1,0:T(8,128)S(1)}, u32[]{:S(2)}, u32[]{:S(2)}) collective-permute-start(f32[264,128]{1,0:T(8,128)S(1)} %get-tuple-element.59), channel_id=1, source_target_pairs={{0,2},{1,3},{2,0},{3,1},{4,6},{5,7},{6,4},{7,5},{8,10},{9,11},{10,... | collective-permute-start | bytes 405512 | tf_op jit(solution)/shard_map/ppermute | solution.py:464
  22.7 6.9 %collective-permute-start.9 = (f32[264,128]{1,0:T(8,128)S(1)}, f32[264,128]{1,0:T(8,128)S(1)}, u32[]{:S(2)}, u32[]{:S(2)}) collective-permute-start(f32[264,128]{1,0:T(8,128)S(1)} %get-tuple-element.57), channel_id=1, source_target_pairs={{0,6},{1,5},{2,4},{3,7},{4,2},{5,1},{6,0},{7,3},{8,14},{9,13},{10,... | collective-permute-start | bytes 405512 | tf_op jit(solution)/shard_map/ppermute | solution.py:464
  29.8 6.4 %collective-permute-start.12 = (f32[2,64,128]{2,1,0:T(8,128)S(1)}, f32[2,64,128]{2,1,0:T(8,128)S(1)}, u32[]{:S(2)}, u32[]{:S(2)}) collective-permute-start(f32[2,64,128]{2,1,0:T(8,128)S(1)} %get-tuple-element.61), channel_id=1, source_target_pairs={{0,24},{8,16},{16,8},{24,0},{1,25},{9,17},{17,9},{25,1},{2,26},{10... | collective-permute-start | bytes 196616 | tf_op jit(solution)/shard_map/ppermute | solution.py:483
  33.5 5.4 %collective-permute-start.13 = (f32[2,64,128]{2,1,0:T(8,128)S(1)}, f32[2,64,128]{2,1,0:T(8,128)S(1)}, u32[]{:S(2)}, u32[]{:S(2)}) collective-permute-start(f32[2,64,128]{2,1,0:T(8,128)S(1)} %get-tuple-element.62), channel_id=1, source_target_pairs={{0,16},{8,24},{16,0},{24,8},{1,17},{9,25},{17,1},{25,9},{2,18},{10... | collective-permute-start | bytes 196616 | tf_op jit(solution)/shard_map/ppermute | solution.py:483
  33.5 5.4 %collective-permute-start.14 = (f32[2,64,128]{2,1,0:T(8,128)S(1)}, f32[2,64,128]{2,1,0:T(8,128)S(1)}, u32[]{:S(2)}, u32[]{:S(2)}) collective-permute-start(f32[2,64,128]{2,1,0:T(8,128)S(1)} %get-tuple-element.63), channel_id=1, source_target_pairs={{0,8},{8,0},{16,24},{24,16},{1,9},{9,1},{17,25},{25,17},{2,10},{10... | collective-permute-start | bytes 196616 | tf_op jit(solution)/shard_map/ppermute | solution.py:483
  38.9 6.2 %collective-permute-start.15 = (f32[2,64,128]{2,1,0:T(8,128)S(1)}, f32[2,64,128]{2,1,0:T(8,128)S(1)}, u32[]{:S(2)}, u32[]{:S(2)}) collective-permute-start(f32[2,64,128]{2,1,0:T(8,128)S(1)} %gradients.1), channel_id=1, source_target_pairs={{0,8},{8,16},{16,24},{24,0},{1,9},{9,17},{17,25},{25,1},{2,10},{10... | collective-permute-start | bytes 196616 | tf_op jit(solution)/shard_map/ppermute | solution.py:499
  39.5 6.8 %collective-permute-start.16 = (f32[2,64,128]{2,1,0:T(8,128)S(1)}, f32[2,64,128]{2,1,0:T(8,128)S(1)}, u32[]{:S(2)}, u32[]{:S(2)}) collective-permute-start(f32[2,64,128]{2,1,0:T(8,128)S(1)} %gradients.1), channel_id=1, source_target_pairs={{0,16},{8,24},{16,0},{24,8},{1,17},{9,25},{17,1},{25,9},{2,18},{10... | collective-permute-start | bytes 196616 | tf_op jit(solution)/shard_map/ppermute | solution.py:499
  41.8 4.5 %collective-permute-start.17 = (f32[2,64,128]{2,1,0:T(8,128)S(1)}, f32[2,64,128]{2,1,0:T(8,128)S(1)}, u32[]{:S(2)}, u32[]{:S(2)}) collective-permute-start(f32[2,64,128]{2,1,0:T(8,128)S(1)} %gradients.1), channel_id=1, source_target_pairs={{0,24},{8,0},{16,8},{24,16},{1,25},{9,1},{17,9},{25,17},{2,26},{10... | collective-permute-start | bytes 196616 | tf_op jit(solution)/shard_map/ppermute | solution.py:499

commit v3 on v2

--- a/solution.py
+++ b/solution.py
@@ -164,8 +164,9 @@
     held = near_speed.shape[0]
     me = lax.axis_index("tile")
     residue, half = lax.rem(me, stripes), lax.div(me, stripes)
+    entries = [entry_of(ref) for ref in lists]
     for hop in range(stripes):
-        entry = entry_of(lists[hop])
+        entry = entries[hop]
         corner, column = lax.div(entry, held), lax.rem(entry, held)
         here = (residue >= corner) == (half == 0)
         piece = outs[hop]
@@ -331,14 +332,18 @@
     me, group = lax.axis_index("tile"), lax.axis_index("grp")
     tile_rows = total.shape[1] // (held + 1)
     part = parts[0].shape[1]
-    total[...] = jnp.zeros_like(total)
+    slots = []
     for pair in came:
         for shot in range(2):
             first = 4 * tile_rows + 4 * shot
-            entry = jnp.max(pair[first : first + 4]).astype(jnp.int32)
+            entry = jnp.max(pair[first : first + 1, :1]).astype(jnp.int32)
             corner, column = lax.div(entry, held), lax.rem(entry, held)
             mine = (corner <= me) & (me < corner + stripes)
-            slot = jnp.where(mine, column, held)
+            slots.append(jnp.where(mine, column, held))
+    total[...] = jnp.zeros_like(total)
+    for index, pair in enumerate(came):
+        for shot in range(2):
+            slot = slots[2 * index + shot]
             rows = pl.ds(pl.multiple_of(slot * tile_rows, tile_rows), tile_rows)
             for field in range(2):
                 first = (2 * shot + field) * tile_rows

time: 47.3 us -> 47.1 us (level)
  no operation moved by 1% of the time
where the time goes in v3:
time: 47.1 us; the launch traced here: 46.9 us
  starting transfers between devices  20.7 us (44%)
  waiting for transfers between devices  17.5 us (37%)
  Pallas kernels  4 us (8%)
  local copies, waits for them, and re-layouts  3.93 us (8%)
  between operations  0.76 us (2%)
    ppermute x9, starting transfers between devices, across(): return lax.ppermute(values, 'tile', [(t, t ^ hop) for t in range(owners)])  7.93 us
    ppermute x3, waiting for transfers between devices, per_device(): lax.ppermute(values, 'tile', [(t, t ^ 2 * hops[t % 2]) for t in range(own...  6.21 us
    ppermute x3, starting transfers between devices, per_device(): lax.ppermute(grads, 'grp', [(g, (g + hop) % groups) for g in range(groups)])  4.8 us
    ppermute x3, waiting for transfers between devices, along(): return lax.ppermute(values, 'grp', [(g, g ^ hop) for g in range(groups)])  4.58 us
    ppermute x3, starting transfers between devices, along(): return lax.ppermute(values, 'grp', [(g, g ^ hop) for g in range(groups)])  4.45 us
    ppermute x9, waiting for transfers between devices, across(): return lax.ppermute(values, 'tile', [(t, t ^ hop) for t in range(owners)])  4.16 us
    ppermute x3, starting transfers between devices, per_device(): lax.ppermute(values, 'tile', [(t, t ^ 2 * hops[t % 2]) for t in range(own...  3.55 us
    unnamed x18, local copies, waits for them, and re-layouts  3.14 us
  transfers between devices with their start and end apart: 18, of which 12 were waited for; matrix products, arithmetic and copies ran while one was open for 0% of the time, Pallas kernels for 3%

profile of v3, /device:TPU:0, one launch (start us, length us, event | category | flops | bytes accessed | tf_op | source)
XLA Modules:
  0.0 46.9 jit_solution(16382200372155671363)
XLA Ops:
  0.6 3.0 %collective-permute-start = (f32[4,2,32,128]{3,2,1,0:T(8,128)}, f32[4,2,32,128]{3,2,1,0:T(8,128)S(1)}, u32[]{:S(2)}, u32[]{:S(2)}) collective-permute-start(f32[4,2,32,128]{3,2,1,0:T(8,128)} %speed.1), channel_id=1, source_target_pairs={{0,4},{1,5},{2,6},{3,7},{4,0},{5,1},{6,2},{7,3},{8,12},{9,13},{10,... | collective-permute-start | bytes 393224 | tf_op jit(solution)/shard_map/ppermute | solution.py:390
  3.7 0.1 collective-permute-start.1
  3.7 0.0 collective-permute-start.2
  3.7 1.9 %collective-permute-start.3 = (s32[1,4]{1,0:T(1,128)}, s32[1,4]{1,0:T(1,128)S(1)}, u32[]{:S(2)}, u32[]{:S(2)}) collective-permute-start(s32[1,4]{1,0:T(1,128)} %aperture.1), channel_id=1, source_target_pairs={{0,2},{1,3},{2,0},{3,1},{4,6},{5,7},{6,4},{7,5},{8,10},{9,11},{10,... | collective-permute-start | bytes 56 | tf_op jit(solution)/shard_map/ppermute | solution.py:390
  5.7 0.2 collective-permute-start.4
  5.8 0.0 copy-start.2
  5.8 0.9 %copy-done.2 = f32[4,2,32,128]{3,2,1,0:T(8,128)S(1)} copy-done((f32[4,2,32,128]{3,2,1,0:T(8,128)S(1)}, f32[4,2,32,128]{3,2,1,0:T(8,128)}, u32[]{:S(2)}) %copy-start.2) | copy-done | bytes 131096
  6.7 0.0 copy-start.3
  6.7 0.9 %copy-done.3 = f32[4,2,32,128]{3,2,1,0:T(8,128)S(1)} copy-done((f32[4,2,32,128]{3,2,1,0:T(8,128)S(1)}, f32[4,2,32,128]{3,2,1,0:T(8,128)}, u32[]{:S(2)}) %copy-start.3) | copy-done | bytes 131096
  7.6 0.0 copy-start.6
  7.6 0.7 %copy-done.6 = s32[1,4]{1,0:T(1,128)S(1)} copy-done((s32[1,4]{1,0:T(1,128)S(1)}, s32[1,4]{1,0:T(1,128)}, u32[]{:S(2)}) %copy-start.6) | copy-done | bytes 40
  8.3 0.1 hold_near_tiles.1
  8.4 0.0 collective-permute-done.2.refs_1_
  8.4 0.0 collective-permute-done.3.refs_2_
  8.4 0.4 collective-permute-done.4.refs_3_
  8.8 0.0 collective-permute-done.far_speed
  8.8 1.4 %collective-permute-done.1.far_density = f32[4,2,32,128]{3,2,1,0:T(8,128)S(1)} collective-permute-done((f32[4,2,32,128]{3,2,1,0:T(8,128)}, f32[4,2,32,128]{3,2,1,0:T(8,128)S(1)}, u32[]{:S(2)}, u32[]{:S(2)}) %collective-permute-start.1) | collective-permute-done | bytes 131104 | tf_op jit(solution)/shard_map/ppermute | solution.py:390
  10.2 0.0 copy-start
  10.2 0.0 copy-start.1
  10.2 0.0 copy-start.8
  10.2 0.1 pick_tiles.1
  10.3 1.8 %collective-permute-start.5 = (f32[2,2,32,128]{3,2,1,0:T(8,128)S(1)}, f32[2,2,32,128]{3,2,1,0:T(8,128)S(1)}, u32[]{:S(2)}, u32[]{:S(2)}) collective-permute-start(f32[2,2,32,128]{3,2,1,0:T(8,128)S(1)} %get-tuple-element.37), channel_id=1, source_target_pairs={{0,2},{1,3},{2,0},{3,1},{4,6},{5,7},{6,4},{7,5},{8,10},{9,11},{10,... | collective-permute-start | bytes 196616 | tf_op jit(solution)/shard_map/ppermute | solution.py:390
  12.1 0.0 collective-permute-start.6
  12.1 0.0 copy-start.4
  12.1 0.4 collective-permute-start.7
  12.5 0.0 copy-start.5
  12.5 0.0 copy-start.7
  12.5 0.0 copy-done
  12.5 0.0 copy-done.1
  12.5 0.0 copy-done.8
  12.5 0.2 copy-done.4
  12.8 0.4 copy-done.5
  13.2 0.0 copy-done.7
  13.2 1.3 %prepare.1 = (f32[3,8,32,128]{3,2,1,0:T(8,128)S(1)}, f32[3,8,32,128]{3,2,1,0:T(8,128)S(1)}, f32[4,8,32,128]{3,2,1,0:T(8,128)S(1)}, f32[4,8,32,128]{3,2,1,0:T(8,1...) custom-call(bf16[1,4,8,32,128]{4,3,2,1,0:T(8,128)(2,1)S(1)} %copy-do, ...), custom_call_target="tpu_custom_call" | custom-call | flops 4000000 | bytes 6000000 | tf_op jit(solution)/shard_map/prepare/pallas_call | solution.py:423
  14.5 0.2 collective-permute-done.5.refs_1_
  14.6 0.0 collective-permute-done.6.refs_2_
  14.6 1.2 %collective-permute-done.7.refs_3_ = f32[2,2,32,128]{3,2,1,0:T(8,128)S(1)} collective-permute-done((f32[2,2,32,128]{3,2,1,0:T(8,128)S(1)}, f32[2,2,32,128]{3,2,1,0:T(8,128)S(1)}, u32[]{:S(2)}, u32[]{:S(2)}) %collective-permute-start.7) | collective-permute-done | bytes 65568 | tf_op jit(solution)/shard_map/ppermute | solution.py:390
  15.8 2.4 %replay_and_adjoint.1 = (f32[2,136,128]{2,1,0:T(8,128)S(1)}, f32[2,136,128]{2,1,0:T(8,128)S(1)}, f32[16,48,128]{2,1,0:T(8,128)S(1)}, f32[16,32,128]{2,1,0:T(8,12...) custom-call(f32[2,2,32,128]{3,2,1,0:T(8,128)S(1)} %get-tuple-element, ...), custom_call_target="tpu_custom_call", output_to_operand_aliasing={{2}: (11, {}), {3}: (12, {}), {4}: (13, {}), {5}: (14, {}),... | custom-call | tf_op jit(solution)/shard_map/replay_and_adjoint/pallas_call | solution.py:440
  18.2 0.5 %collective-permute-start.8 = (f32[2,136,128]{2,1,0:T(8,128)S(1)}, f32[2,136,128]{2,1,0:T(8,128)S(1)}, u32[]{:S(2)}, u32[]{:S(2)}) collective-permute-start(f32[2,136,128]{2,1,0:T(8,128)S(1)} %get-tuple-element.55), channel_id=1, source_target_pairs={{0,1},{1,0},{2,3},{3,2},{4,5},{5,4},{6,7},{7,6},{8,9},{9,8},{10,11... | collective-permute-start | bytes 417800 | tf_op jit(solution)/shard_map/ppermute | solution.py:390
  18.7 1.0 %collective-permute-done.8.came = f32[2,136,128]{2,1,0:T(8,128)S(1)} collective-permute-done((f32[2,136,128]{2,1,0:T(8,128)S(1)}, f32[2,136,128]{2,1,0:T(8,128)S(1)}, u32[]{:S(2)}, u32[]{:S(2)}) %collective-permute-start.8) | collective-permute-done | bytes 139296 | tf_op jit(solution)/shard_map/ppermute | solution.py:390
  19.8 1.6 %collective-permute-start.10 = (f32[264,128]{1,0:T(8,128)S(1)}, f32[264,128]{1,0:T(8,128)S(1)}, u32[]{:S(2)}, u32[]{:S(2)}) collective-permute-start(f32[264,128]{1,0:T(8,128)S(1)} %get-tuple-element.58), channel_id=1, source_target_pairs={{0,4},{1,7},{2,6},{3,5},{4,0},{5,3},{6,2},{7,1},{8,12},{9,15},{10,... | collective-permute-start | bytes 405512 | tf_op jit(solution)/shard_map/ppermute | solution.py:469
  21.3 1.2 %collective-permute-start.11 = (f32[264,128]{1,0:T(8,128)S(1)}, f32[264,128]{1,0:T(8,128)S(1)}, u32[]{:S(2)}, u32[]{:S(2)}) collective-permute-start(f32[264,128]{1,0:T(8,128)S(1)} %get-tuple-element.59), channel_id=1, source_target_pairs={{0,2},{1,3},{2,0},{3,1},{4,6},{5,7},{6,4},{7,5},{8,10},{9,11},{10,... | collective-permute-start | bytes 405512 | tf_op jit(solution)/shard_map/ppermute | solution.py:469
  22.6 0.7 %collective-permute-start.9 = (f32[264,128]{1,0:T(8,128)S(1)}, f32[264,128]{1,0:T(8,128)S(1)}, u32[]{:S(2)}, u32[]{:S(2)}) collective-permute-start(f32[264,128]{1,0:T(8,128)S(1)} %get-tuple-element.57), channel_id=1, source_target_pairs={{0,6},{1,5},{2,4},{3,7},{4,2},{5,1},{6,0},{7,3},{8,14},{9,13},{10,... | collective-permute-start | bytes 405512 | tf_op jit(solution)/shard_map/ppermute | solution.py:469
  23.3 3.8 %collective-permute-done.10.refs_2_ = f32[264,128]{1,0:T(8,128)S(1)} collective-permute-done((f32[264,128]{1,0:T(8,128)S(1)}, f32[264,128]{1,0:T(8,128)S(1)}, u32[]{:S(2)}, u32[]{:S(2)}) %collective-permute-start.10) | collective-permute-done | bytes 135200 | tf_op jit(solution)/shard_map/ppermute | solution.py:469
  27.1 0.7 %collective-permute-done.11.refs_3_ = f32[264,128]{1,0:T(8,128)S(1)} collective-permute-done((f32[264,128]{1,0:T(8,128)S(1)}, f32[264,128]{1,0:T(8,128)S(1)}, u32[]{:S(2)}, u32[]{:S(2)}) %collective-permute-start.11) | collective-permute-done | bytes 135200 | tf_op jit(solution)/shard_map/ppermute | solution.py:469
  27.8 1.7 %collective-permute-done.9.refs_1_ = f32[264,128]{1,0:T(8,128)S(1)} collective-permute-done((f32[264,128]{1,0:T(8,128)S(1)}, f32[264,128]{1,0:T(8,128)S(1)}, u32[]{:S(2)}, u32[]{:S(2)}) %collective-permute-start.9) | collective-permute-done | bytes 135200 | tf_op jit(solution)/shard_map/ppermute | solution.py:469
  29.5 0.1 add_stripes.1
  29.7 3.7 %collective-permute-start.12 = (f32[2,64,128]{2,1,0:T(8,128)S(1)}, f32[2,64,128]{2,1,0:T(8,128)S(1)}, u32[]{:S(2)}, u32[]{:S(2)}) collective-permute-start(f32[2,64,128]{2,1,0:T(8,128)S(1)} %get-tuple-element.61), channel_id=1, source_target_pairs={{0,24},{8,16},{16,8},{24,0},{1,25},{9,17},{17,9},{25,1},{2,26},{10... | collective-permute-start | bytes 196616 | tf_op jit(solution)/shard_map/ppermute | solution.py:488
  33.3 0.0 collective-permute-start.13
  33.3 0.8 %collective-permute-start.14 = (f32[2,64,128]{2,1,0:T(8,128)S(1)}, f32[2,64,128]{2,1,0:T(8,128)S(1)}, u32[]{:S(2)}, u32[]{:S(2)}) collective-permute-start(f32[2,64,128]{2,1,0:T(8,128)S(1)} %get-tuple-element.63), channel_id=1, source_target_pairs={{0,8},{8,0},{16,24},{24,16},{1,9},{9,1},{17,25},{25,17},{2,10},{10... | collective-permute-start | bytes 196616 | tf_op jit(solution)/shard_map/ppermute | solution.py:488
  34.1 2.0 %collective-permute-done.12.refs_1_ = f32[2,64,128]{2,1,0:T(8,128)S(1)} collective-permute-done((f32[2,64,128]{2,1,0:T(8,128)S(1)}, f32[2,64,128]{2,1,0:T(8,128)S(1)}, u32[]{:S(2)}, u32[]{:S(2)}) %collective-permute-start.12) | collective-permute-done | bytes 65568 | tf_op jit(solution)/shard_map/ppermute | solution.py:488
  36.1 2.6 %collective-permute-done.13.refs_2_ = f32[2,64,128]{2,1,0:T(8,128)S(1)} collective-permute-done((f32[2,64,128]{2,1,0:T(8,128)S(1)}, f32[2,64,128]{2,1,0:T(8,128)S(1)}, u32[]{:S(2)}, u32[]{:S(2)}) %collective-permute-start.13) | collective-permute-done | bytes 65568 | tf_op jit(solution)/shard_map/ppermute | solution.py:488
  38.7 0.0 collective-permute-done.14.refs_3_
  38.7 0.6 %collective-permute-start.15 = (f32[2,64,128]{2,1,0:T(8,128)S(1)}, f32[2,64,128]{2,1,0:T(8,128)S(1)}, u32[]{:S(2)}, u32[]{:S(2)}) collective-permute-start(f32[2,64,128]{2,1,0:T(8,128)S(1)} %gradients.1), channel_id=1, source_target_pairs={{0,8},{8,16},{16,24},{24,0},{1,9},{9,17},{17,25},{25,1},{2,10},{10... | collective-permute-start | bytes 196616 | tf_op jit(solution)/shard_map/ppermute | solution.py:504
  39.3 2.3 %collective-permute-start.16 = (f32[2,64,128]{2,1,0:T(8,128)S(1)}, f32[2,64,128]{2,1,0:T(8,128)S(1)}, u32[]{:S(2)}, u32[]{:S(2)}) collective-permute-start(f32[2,64,128]{2,1,0:T(8,128)S(1)} %gradients.1), channel_id=1, source_target_pairs={{0,16},{8,24},{16,0},{24,8},{1,17},{9,25},{17,1},{25,9},{2,18},{10... | collective-permute-start | bytes 196616 | tf_op jit(solution)/shard_map/ppermute | solution.py:504
  41.6 1.9 %collective-permute-start.17 = (f32[2,64,128]{2,1,0:T(8,128)S(1)}, f32[2,64,128]{2,1,0:T(8,128)S(1)}, u32[]{:S(2)}, u32[]{:S(2)}) collective-permute-start(f32[2,64,128]{2,1,0:T(8,128)S(1)} %gradients.1), channel_id=1, source_target_pairs={{0,24},{8,0},{16,8},{24,16},{1,25},{9,1},{17,9},{25,17},{2,26},{10... | collective-permute-start | bytes 196616 | tf_op jit(solution)/shard_map/ppermute | solution.py:504
  43.6 1.4 %collective-permute-done.15 = f32[2,64,128]{2,1,0:T(8,128)S(1)} collective-permute-done((f32[2,64,128]{2,1,0:T(8,128)S(1)}, f32[2,64,128]{2,1,0:T(8,128)S(1)}, u32[]{:S(2)}, u32[]{:S(2)}) %collective-permute-start.15) | collective-permute-done | bytes 65568 | tf_op jit(solution)/shard_map/ppermute | solution.py:504
  45.0 1.2 %collective-permute-done.16 = f32[2,64,128]{2,1,0:T(8,128)S(1)} collective-permute-done((f32[2,64,128]{2,1,0:T(8,128)S(1)}, f32[2,64,128]{2,1,0:T(8,128)S(1)}, u32[]{:S(2)}, u32[]{:S(2)}) %collective-permute-start.16) | collective-permute-done | bytes 65568 | tf_op jit(solution)/shard_map/ppermute | solution.py:504
  46.2 0.0 collective-permute-done.17
  46.2 0.7 %fusion = (f32[1,4,64,128]{3,2,1,0:T(8,128)}, f32[1,4,64,128]{3,2,1,0:T(8,128)}) fusion(f32[2,4,64,128]{3,2,1,0:T(8,128)S(1)} %bitcast_dynamic-update-slice_fusion), kind=kLoop, calls=%fused_computation.4 | loop fusion | bytes 524288 | tf_op jit(solution)/shard_map/slice | solution.py:507
  (8 shorter events, 0.1 us)
Async XLA Ops:
  0.6 8.1 %collective-permute-start = (f32[4,2,32,128]{3,2,1,0:T(8,128)}, f32[4,2,32,128]{3,2,1,0:T(8,128)S(1)}, u32[]{:S(2)}, u32[]{:S(2)}) collective-permute-start(f32[4,2,32,128]{3,2,1,0:T(8,128)} %speed.1), channel_id=1, source_target_pairs={{0,4},{1,5},{2,6},{3,7},{4,0},{5,1},{6,2},{7,3},{8,12},{9,13},{10,... | collective-permute-start | bytes 393224 | tf_op jit(solution)/shard_map/ppermute | solution.py:390
  3.7 6.5 %collective-permute-start.1 = (f32[4,2,32,128]{3,2,1,0:T(8,128)}, f32[4,2,32,128]{3,2,1,0:T(8,128)S(1)}, u32[]{:S(2)}, u32[]{:S(2)}) collective-permute-start(f32[4,2,32,128]{3,2,1,0:T(8,128)} %density.1), channel_id=1, source_target_pairs={{0,4},{1,5},{2,6},{3,7},{4,0},{5,1},{6,2},{7,3},{8,12},{9,13},{10,... | collective-permute-start | bytes 393224 | tf_op jit(solution)/shard_map/ppermute | solution.py:390
  3.7 4.6 %collective-permute-start.2 = (s32[1,4]{1,0:T(1,128)}, s32[1,4]{1,0:T(1,128)S(1)}, u32[]{:S(2)}, u32[]{:S(2)}) collective-permute-start(s32[1,4]{1,0:T(1,128)} %aperture.1), channel_id=1, source_target_pairs={{0,1},{1,0},{2,3},{3,2},{4,5},{5,4},{6,7},{7,6},{8,9},{9,8},{10,11... | collective-permute-start | bytes 56 | tf_op jit(solution)/shard_map/ppermute | solution.py:390
  3.7 4.6 %collective-permute-start.3 = (s32[1,4]{1,0:T(1,128)}, s32[1,4]{1,0:T(1,128)S(1)}, u32[]{:S(2)}, u32[]{:S(2)}) collective-permute-start(s32[1,4]{1,0:T(1,128)} %aperture.1), channel_id=1, source_target_pairs={{0,2},{1,3},{2,0},{3,1},{4,6},{5,7},{6,4},{7,5},{8,10},{9,11},{10,... | collective-permute-start | bytes 56 | tf_op jit(solution)/shard_map/ppermute | solution.py:390
  5.7 3.1 %collective-permute-start.4 = (s32[1,4]{1,0:T(1,128)}, s32[1,4]{1,0:T(1,128)S(1)}, u32[]{:S(2)}, u32[]{:S(2)}) collective-permute-start(s32[1,4]{1,0:T(1,128)} %aperture.1), channel_id=1, source_target_pairs={{0,3},{1,2},{2,1},{3,0},{4,7},{5,6},{6,5},{7,4},{8,11},{9,10},{10,... | collective-permute-start | bytes 56 | tf_op jit(solution)/shard_map/ppermute | solution.py:390
  5.8 0.9 %copy-start.2 = (f32[4,2,32,128]{3,2,1,0:T(8,128)S(1)}, f32[4,2,32,128]{3,2,1,0:T(8,128)}, u32[]{:S(2)}) copy-start(f32[4,2,32,128]{3,2,1,0:T(8,128)} %speed.1) | copy-start | bytes 393220
  6.7 0.9 %copy-start.3 = (f32[4,2,32,128]{3,2,1,0:T(8,128)S(1)}, f32[4,2,32,128]{3,2,1,0:T(8,128)}, u32[]{:S(2)}) copy-start(f32[4,2,32,128]{3,2,1,0:T(8,128)} %density.1) | copy-start | bytes 393220
  7.6 0.7 %copy-start.6 = (s32[1,4]{1,0:T(1,128)S(1)}, s32[1,4]{1,0:T(1,128)}, u32[]{:S(2)}) copy-start(s32[1,4]{1,0:T(1,128)} %aperture.1) | copy-start | bytes 52
  10.2 2.3 %copy-start = (bf16[1,4,8,32,128]{4,3,2,1,0:T(8,128)(2,1)S(1)}, bf16[1,4,8,32,128]{4,3,2,1,0:T(8,128)(2,1)}, u32[]{:S(2)}) copy-start(bf16[1,4,8,32,128]{4,3,2,1,0:T(8,128)(2,1)} %fwd.1) | copy-start | bytes 786436
  10.2 2.3 %copy-start.1 = (bf16[1,4,8,32,128]{4,3,2,1,0:T(8,128)(2,1)S(1)}, bf16[1,4,8,32,128]{4,3,2,1,0:T(8,128)(2,1)}, u32[]{:S(2)}) copy-start(bf16[1,4,8,32,128]{4,3,2,1,0:T(8,128)(2,1)} %adj.1) | copy-start | bytes 786436
  10.2 2.3 %copy-start.8 = (f32[1,4]{1,0:T(1,128)S(1)}, f32[1,4]{1,0:T(1,128)}, u32[]{:S(2)}) copy-start(f32[1,4]{1,0:T(1,128)} %wave.1) | copy-start | bytes 52
  10.3 4.3 %collective-permute-start.5 = (f32[2,2,32,128]{3,2,1,0:T(8,128)S(1)}, f32[2,2,32,128]{3,2,1,0:T(8,128)S(1)}, u32[]{:S(2)}, u32[]{:S(2)}) collective-permute-start(f32[2,2,32,128]{3,2,1,0:T(8,128)S(1)} %get-tuple-element.37), channel_id=1, source_target_pairs={{0,2},{1,3},{2,0},{3,1},{4,6},{5,7},{6,4},{7,5},{8,10},{9,11},{10,... | collective-permute-start | bytes 196616 | tf_op jit(solution)/shard_map/ppermute | solution.py:390
  12.1 2.6 %collective-permute-start.6 = (f32[2,2,32,128]{3,2,1,0:T(8,128)S(1)}, f32[2,2,32,128]{3,2,1,0:T(8,128)S(1)}, u32[]{:S(2)}, u32[]{:S(2)}) collective-permute-start(f32[2,2,32,128]{3,2,1,0:T(8,128)S(1)} %get-tuple-element.38), channel_id=1, source_target_pairs={{0,1},{1,0},{2,3},{3,2},{4,5},{5,4},{6,7},{7,6},{8,9},{9,8},{10,11... | collective-permute-start | bytes 196616 | tf_op jit(solution)/shard_map/ppermute | solution.py:390
  12.1 0.7 %copy-start.4 = (f32[1,4,8]{2,1,0:T(4,128)S(1)}, f32[1,4,8]{2,1,0:T(4,128)}, u32[]{:S(2)}) copy-start(f32[1,4,8]{2,1,0:T(4,128)} %res.1) | copy-start | bytes 388
  12.1 3.7 %collective-permute-start.7 = (f32[2,2,32,128]{3,2,1,0:T(8,128)S(1)}, f32[2,2,32,128]{3,2,1,0:T(8,128)S(1)}, u32[]{:S(2)}, u32[]{:S(2)}) collective-permute-start(f32[2,2,32,128]{3,2,1,0:T(8,128)S(1)} %get-tuple-element.39), channel_id=1, source_target_pairs={{0,3},{1,2},{2,1},{3,0},{4,7},{5,6},{6,5},{7,4},{8,11},{9,10},{10,... | collective-permute-start | bytes 196616 | tf_op jit(solution)/shard_map/ppermute | solution.py:390
  12.5 0.7 %copy-start.5 = (s32[1,8,2]{1,2,0:T(2,128)S(1)}, s32[1,8,2]{1,2,0:T(2,128)}, u32[]{:S(2)}) copy-start(s32[1,8,2]{1,2,0:T(2,128)} %param.16) | copy-start | bytes 196
  12.5 0.7 %copy-start.7 = (s32[1,3]{1,0:T(1,128)S(1)}, s32[1,3]{1,0:T(1,128)}, u32[]{:S(2)}) copy-start(s32[1,3]{1,0:T(1,128)} %src.1) | copy-start | bytes 40
  18.2 1.5 %collective-permute-start.8 = (f32[2,136,128]{2,1,0:T(8,128)S(1)}, f32[2,136,128]{2,1,0:T(8,128)S(1)}, u32[]{:S(2)}, u32[]{:S(2)}) collective-permute-start(f32[2,136,128]{2,1,0:T(8,128)S(1)} %get-tuple-element.55), channel_id=1, source_target_pairs={{0,1},{1,0},{2,3},{3,2},{4,5},{5,4},{6,7},{7,6},{8,9},{9,8},{10,11... | collective-permute-start | bytes 417800 | tf_op jit(solution)/shard_map/ppermute | solution.py:390
  19.8 7.4 %collective-permute-start.10 = (f32[264,128]{1,0:T(8,128)S(1)}, f32[264,128]{1,0:T(8,128)S(1)}, u32[]{:S(2)}, u32[]{:S(2)}) collective-permute-start(f32[264,128]{1,0:T(8,128)S(1)} %get-tuple-element.58), channel_id=1, source_target_pairs={{0,4},{1,7},{2,6},{3,5},{4,0},{5,3},{6,2},{7,1},{8,12},{9,15},{10,... | collective-permute-start | bytes 405512 | tf_op jit(solution)/shard_map/ppermute | solution.py:469
  21.3 6.5 %collective-permute-start.11 = (f32[264,128]{1,0:T(8,128)S(1)}, f32[264,128]{1,0:T(8,128)S(1)}, u32[]{:S(2)}, u32[]{:S(2)}) collective-permute-start(f32[264,128]{1,0:T(8,128)S(1)} %get-tuple-element.59), channel_id=1, source_target_pairs={{0,2},{1,3},{2,0},{3,1},{4,6},{5,7},{6,4},{7,5},{8,10},{9,11},{10,... | collective-permute-start | bytes 405512 | tf_op jit(solution)/shard_map/ppermute | solution.py:469
  22.6 6.9 %collective-permute-start.9 = (f32[264,128]{1,0:T(8,128)S(1)}, f32[264,128]{1,0:T(8,128)S(1)}, u32[]{:S(2)}, u32[]{:S(2)}) collective-permute-start(f32[264,128]{1,0:T(8,128)S(1)} %get-tuple-element.57), channel_id=1, source_target_pairs={{0,6},{1,5},{2,4},{3,7},{4,2},{5,1},{6,0},{7,3},{8,14},{9,13},{10,... | collective-permute-start | bytes 405512 | tf_op jit(solution)/shard_map/ppermute | solution.py:469
  29.7 6.4 %collective-permute-start.12 = (f32[2,64,128]{2,1,0:T(8,128)S(1)}, f32[2,64,128]{2,1,0:T(8,128)S(1)}, u32[]{:S(2)}, u32[]{:S(2)}) collective-permute-start(f32[2,64,128]{2,1,0:T(8,128)S(1)} %get-tuple-element.61), channel_id=1, source_target_pairs={{0,24},{8,16},{16,8},{24,0},{1,25},{9,17},{17,9},{25,1},{2,26},{10... | collective-permute-start | bytes 196616 | tf_op jit(solution)/shard_map/ppermute | solution.py:488
  33.3 5.4 %collective-permute-start.13 = (f32[2,64,128]{2,1,0:T(8,128)S(1)}, f32[2,64,128]{2,1,0:T(8,128)S(1)}, u32[]{:S(2)}, u32[]{:S(2)}) collective-permute-start(f32[2,64,128]{2,1,0:T(8,128)S(1)} %get-tuple-element.62), channel_id=1, source_target_pairs={{0,16},{8,24},{16,0},{24,8},{1,17},{9,25},{17,1},{25,9},{2,18},{10... | collective-permute-start | bytes 196616 | tf_op jit(solution)/shard_map/ppermute | solution.py:488
  33.3 5.4 %collective-permute-start.14 = (f32[2,64,128]{2,1,0:T(8,128)S(1)}, f32[2,64,128]{2,1,0:T(8,128)S(1)}, u32[]{:S(2)}, u32[]{:S(2)}) collective-permute-start(f32[2,64,128]{2,1,0:T(8,128)S(1)} %get-tuple-element.63), channel_id=1, source_target_pairs={{0,8},{8,0},{16,24},{24,16},{1,9},{9,1},{17,25},{25,17},{2,10},{10... | collective-permute-start | bytes 196616 | tf_op jit(solution)/shard_map/ppermute | solution.py:488
  38.7 6.2 %collective-permute-start.15 = (f32[2,64,128]{2,1,0:T(8,128)S(1)}, f32[2,64,128]{2,1,0:T(8,128)S(1)}, u32[]{:S(2)}, u32[]{:S(2)}) collective-permute-start(f32[2,64,128]{2,1,0:T(8,128)S(1)} %gradients.1), channel_id=1, source_target_pairs={{0,8},{8,16},{16,24},{24,0},{1,9},{9,17},{17,25},{25,1},{2,10},{10... | collective-permute-start | bytes 196616 | tf_op jit(solution)/shard_map/ppermute | solution.py:504
  39.3 6.8 %collective-permute-start.16 = (f32[2,64,128]{2,1,0:T(8,128)S(1)}, f32[2,64,128]{2,1,0:T(8,128)S(1)}, u32[]{:S(2)}, u32[]{:S(2)}) collective-permute-start(f32[2,64,128]{2,1,0:T(8,128)S(1)} %gradients.1), channel_id=1, source_target_pairs={{0,16},{8,24},{16,0},{24,8},{1,17},{9,25},{17,1},{25,9},{2,18},{10... | collective-permute-start | bytes 196616 | tf_op jit(solution)/shard_map/ppermute | solution.py:504
  41.6 4.5 %collective-permute-start.17 = (f32[2,64,128]{2,1,0:T(8,128)S(1)}, f32[2,64,128]{2,1,0:T(8,128)S(1)}, u32[]{:S(2)}, u32[]{:S(2)}) collective-permute-start(f32[2,64,128]{2,1,0:T(8,128)S(1)} %gradients.1), channel_id=1, source_target_pairs={{0,24},{8,0},{16,8},{24,16},{1,25},{9,1},{17,9},{25,17},{2,26},{10... | collective-permute-start | bytes 196616 | tf_op jit(solution)/shard_map/ppermute | solution.py:504
